TPU v7x, 32 devices: a whole 2x2x4 slice. The times are simulated.
32 devices in a mesh: dp: 16 (over z, x, core), seq: 2 (over y).
Axes of the slice: x: 2, y: 2, z: 4, core: 2. Of those that a mesh axis runs over, the one named last changes fastest.
Arguments:
- frames: bfloat16 [16, 512, 1024], P('dp', 'seq'), may hold values from -6 to 6
- cotangent: bfloat16 [16, 512, 1024], P('dp', 'seq'), may hold values from -6 to 6
- clip_lengths: int32 [16, 2], P('dp'), may hold values from 1 to 400, 512 in all within a row
- params: float32 [16783360], P(('dp', 'seq')), may hold values from -1.5 to 1.5
- first_moment: float32 [16783360], P(('dp', 'seq')), may hold values from -6 to 6
- second_moment: float32 [16783360], P(('dp', 'seq')), may hold values from 0.1 to 10
Outputs:
- output: bfloat16 [16, 512, 1024], P('dp', 'seq')
- frames_grad: bfloat16 [16, 512, 1024], P('dp', 'seq')
- params_grad: float32 [16783360], P(('dp', 'seq'))
- new_params: float32 [16783360], P(('dp', 'seq'))
- new_first: float32 [16783360], P(('dp', 'seq'))
- new_second: float32 [16783360], P(('dp', 'seq'))
Inputs may be any that keep to these rules, and one draw needn't show every extreme that they name: `clip_lengths`: row b lists in order the lengths of the clips packed into sequence b; its last entry counts the padding frames at the end. Each row sums to 512 and no entry exceeds 400.
All inputs are finite; a program needn't handle non-finite values.
Results may differ from a plain program's by a relative error of at most 0.012.
The roundings to bfloat16 on the way count: a program that leaves them out, or rounds other values in their place, can miss the bound.
Values may be sent and summed in bfloat16 or wider, within the bound.
No kernel may reach another device: no remote copies, remote signals or barrier semaphores. Data moves between devices by JAX's collectives and lax.ppermute only.
A program may use at most 256 MiB of HBM per device.

v0:
```python
import functools
import math

import jax
import jax.numpy as jnp
import numpy as np
from jax import lax
from jax.experimental import pallas as pl
from jax.experimental.pallas import tpu as pltpu
from jax.sharding import Mesh
from jax.sharding import PartitionSpec as P

D = 1024
HEADS = 16
HEAD_DIM = 64
FF = 4096
WINDOW = 128


eps_norm = 1e-05
beta_one = 0.9
beta_two = 0.99
learn_rate = 0.01
decay_rate = 0.1
eps_adam = 1e-08
adam_step = 100.0
neg_large = -1e30
rope_base = 10000.0


def padded(shard, sides, width):
    for axis, dim in sides:
        size, length = (lax.axis_size(axis), shard.shape[dim])
        up = [(i, (i + 1) % size) for i in range(size - 1)]
        down = [(j, i) for i, j in up]
        last = lax.slice_in_dim(shard, length - width, length, axis=dim)
        first = lax.slice_in_dim(shard, 0, width, axis=dim)
        before = lax.ppermute(last, axis, up)
        after = lax.ppermute(first, axis, down)
        shard = jnp.concatenate([before, shard, after], axis=dim)
    return shard


def unpack(flat_params):
    end_qkv = D * 3 * D
    end_out = end_qkv + D * D
    end_mlp = end_out + D * 2 * FF
    end_down = end_mlp + FF * D
    w_qkv = flat_params[:end_qkv].reshape(D, 3 * D)
    w_out = flat_params[end_qkv:end_out].reshape(D, D)
    w_gate_up = flat_params[end_out:end_mlp].reshape(D, 2 * FF)
    w_down = flat_params[end_mlp:end_down].reshape(FF, D)
    vectors = flat_params[end_down:].reshape(6, D).astype(jnp.float32)
    return (w_qkv, w_out, w_gate_up, w_down, vectors)


def clip_info(lengths, glob):
    clip_ends = jnp.cumsum(lengths, axis=1, dtype=jnp.int32)
    clip_starts = clip_ends - lengths
    after_end = (glob[None, :, None] >= clip_ends[:, None, :]).astype(jnp.int32)
    segment = jnp.sum(after_end, axis=2, dtype=jnp.int32)
    onehot = segment[:, :, None] == jnp.arange(lengths.shape[1], dtype=jnp.int32)[None, None, :]
    clip_begin = jnp.sum(jnp.where(onehot, clip_starts[:, None, :], 0), axis=2, dtype=jnp.int32)
    return (segment, (glob[None, :] - clip_begin).astype(jnp.float32))


def rotate(values, position, sign):
    half_dim = values.shape[-1] // 2
    inverse = jnp.exp(
        jnp.arange(half_dim, dtype=jnp.float32) * (-2.0 * math.log(rope_base) / HEAD_DIM)
    )
    rot_angle = position[:, :, None, None] * inverse
    cosine = jnp.cos(rot_angle)
    rot_sine = sign * jnp.sin(rot_angle)
    low_half = values[..., :half_dim]
    high_half = values[..., half_dim:]
    return jnp.concatenate(
        [low_half * cosine - high_half * rot_sine, high_half * cosine + low_half * rot_sine],
        axis=-1,
    )


def norm_forward(row_vals, norm_gain, norm_bias):
    centered = row_vals - jnp.mean(row_vals, axis=-1, keepdims=True)
    inv_scale = lax.rsqrt(jnp.mean(centered * centered, axis=-1, keepdims=True) + eps_norm)
    normed = centered * inv_scale
    return (normed * norm_gain + norm_bias, normed, inv_scale)


def norm_backward(out_grad, normed, inv_scale, norm_gain):
    d_gain = jnp.sum(out_grad * normed, axis=0)
    d_bias = jnp.sum(out_grad, axis=0)
    inner_grad = out_grad * norm_gain
    d_rows = inv_scale * (
        inner_grad
        - jnp.mean(inner_grad, axis=-1, keepdims=True)
        - normed * jnp.mean(inner_grad * normed, axis=-1, keepdims=True)
    )
    return (d_rows, d_gain, d_bias)


def scores_of(query_rows, key_rows, window_mask):
    raw_scores = jnp.einsum(
        "qhd,khd->hqk", query_rows, key_rows, preferred_element_type=jnp.float32
    ) * HEAD_DIM ** (-0.5)
    return jnp.where(window_mask[None], raw_scores, neg_large)


def attend(query_rows, key_rows, value_rows, window_mask):
    masked = scores_of(query_rows, key_rows, window_mask)
    row_max = jnp.max(masked, axis=-1, keepdims=True)
    row_total = jnp.log(jnp.sum(jnp.exp(masked - row_max), axis=-1, keepdims=True)) + row_max
    prob_low = jnp.exp(masked - row_total).astype(jnp.bfloat16)
    attn_rows = jnp.einsum("hqk,khd->qhd", prob_low, value_rows, preferred_element_type=jnp.float32)
    return (attn_rows, row_total[..., 0])


def attend_back(query_rows, key_rows, value_rows, window_mask, row_total, d_attn):
    masked = scores_of(query_rows, key_rows, window_mask)
    prob_rows = jnp.exp(masked - row_total[..., None])
    prob_low = prob_rows.astype(jnp.bfloat16)
    d_values = jnp.einsum("hqk,qhd->khd", prob_low, d_attn, preferred_element_type=jnp.float32)
    d_probs = jnp.einsum("qhd,khd->hqk", d_attn, value_rows, preferred_element_type=jnp.float32)
    inner_sum = jnp.sum(prob_rows * d_probs, axis=-1, keepdims=True)
    d_scores = (prob_rows * (d_probs - inner_sum)).astype(jnp.bfloat16)
    d_query = jnp.einsum(
        "hqk,khd->qhd", d_scores, key_rows, preferred_element_type=jnp.float32
    ) * HEAD_DIM ** (-0.5)
    d_keys = jnp.einsum(
        "hqk,qhd->khd", d_scores, query_rows, preferred_element_type=jnp.float32
    ) * HEAD_DIM ** (-0.5)
    return (d_query, d_keys, d_values)


def adam_update(flat_params, grads, first_moment, second_moment):
    new_first = beta_one * first_moment + (1.0 - beta_one) * grads
    new_second = beta_two * second_moment + (1.0 - beta_two) * grads * grads
    corrected_first = new_first / (1.0 - beta_one**adam_step)
    corrected_second = new_second / (1.0 - beta_two**adam_step)
    step_size = corrected_first / (jnp.sqrt(corrected_second) + eps_adam) + decay_rate * flat_params
    return (flat_params - learn_rate * step_size, new_first, new_second)


def body(frames, cotangent, clip_lengths, params, first_moment, second_moment):
    seq_count, frame_span, model_width = frames.shape
    row_count = seq_count * frame_span
    window_reach = WINDOW
    key_count = frame_span + 2 * window_reach
    head_count = HEADS
    head_size = model_width // head_count
    group_size = 4
    seq_len = lax.axis_size("seq") * frame_span
    seq_start = lax.axis_index("seq") * frame_span
    glob_rows = seq_start + jnp.arange(frame_span, dtype=jnp.int32)
    glob_keys = seq_start - window_reach + jnp.arange(key_count, dtype=jnp.int32)
    seg_rows, pos_rows = clip_info(clip_lengths, glob_rows)
    seg_keys, unused = clip_info(clip_lengths, glob_keys)
    inside = (glob_keys >= 0) & (glob_keys < seq_len)
    near_band = (
        jnp.abs(jnp.arange(frame_span)[:, None] + window_reach - jnp.arange(key_count)[None, :])
        < window_reach
    )
    window_mask = (
        (seg_rows[:, :, None] == seg_keys[:, None, :]) & inside[None, None, :] & near_band[None]
    )
    keep_rows = seg_rows != clip_lengths.shape[1] - 1
    shards = params.astype(jnp.bfloat16)
    gathered = lax.all_gather(shards, ("dp", "seq"), axis=0, tiled=True)
    w_qkv, w_out, w_gate_up, w_down, vectors = unpack(gathered)
    x_rows = frames.reshape(row_count, model_width).astype(jnp.float32)
    norm_one, normed_one, scale_one = norm_forward(x_rows, vectors[0], vectors[1])
    a_low = norm_one.astype(jnp.bfloat16)
    qkv = jnp.dot(a_low, w_qkv, preferred_element_type=jnp.float32).reshape(
        seq_count, frame_span, 3, head_count, head_size
    )
    query_low = rotate(qkv[:, :, 0], pos_rows, 1.0).astype(jnp.bfloat16)
    key_low = rotate(qkv[:, :, 1], pos_rows, 1.0).astype(jnp.bfloat16)
    value_low = qkv[:, :, 2].astype(jnp.bfloat16)
    key_value = jnp.concatenate([key_low, value_low], axis=2).reshape(
        seq_count, frame_span, 2 * model_width
    )
    wide_rows = padded(key_value, (("seq", 1),), window_reach)
    wide_rows = wide_rows.reshape(seq_count, key_count, 2, head_count, head_size)
    key_wide = wide_rows[:, :, 0]
    value_wide = wide_rows[:, :, 1]
    seq_index = 0
    out_parts = []
    total_parts = []
    for head_start in range(0, head_count, group_size):
        head_end = head_start + group_size
        attn_rows, row_total = attend(
            query_low[seq_index, :, head_start:head_end],
            key_wide[seq_index, :, head_start:head_end],
            value_wide[seq_index, :, head_start:head_end],
            window_mask[seq_index],
        )
        out_parts.append(attn_rows)
        total_parts.append(row_total)
    attn_list = [jnp.concatenate(out_parts, axis=1)]
    total_list = [total_parts]
    attn_all = jnp.where(keep_rows[:, :, None, None], jnp.stack(attn_list), 0.0)
    attn_low = attn_all.reshape(row_count, model_width).astype(jnp.bfloat16)
    branch_attn = jnp.dot(attn_low, w_out, preferred_element_type=jnp.float32)
    mid_rows = x_rows + vectors[4] * branch_attn
    norm_two, normed_two, scale_two = norm_forward(mid_rows, vectors[2], vectors[3])
    c_low = norm_two.astype(jnp.bfloat16)
    gate_up = jnp.dot(c_low, w_gate_up, preferred_element_type=jnp.float32)
    gate = gate_up[:, :FF]
    up_rows = gate_up[:, FF:]
    gate_sig = jax.nn.sigmoid(gate)
    hidden = (gate * gate_sig * up_rows).astype(jnp.bfloat16)
    branch_mlp = jnp.dot(hidden, w_down, preferred_element_type=jnp.float32)
    output = (
        (mid_rows + vectors[5] * branch_mlp)
        .astype(jnp.bfloat16)
        .reshape(seq_count, frame_span, model_width)
    )
    gathered = lax.all_gather(shards, ("dp", "seq"), axis=0, tiled=True)
    w_qkv, w_out, w_gate_up, w_down, vectors = unpack(gathered)
    d_rows = cotangent.reshape(row_count, model_width).astype(jnp.float32)
    g_scale_mlp = jnp.sum(d_rows * branch_mlp, axis=0)
    d_mlp = (d_rows * vectors[5]).astype(jnp.bfloat16)
    g_down = jnp.dot(hidden.T, d_mlp, preferred_element_type=jnp.float32)
    d_hidden = jnp.dot(d_mlp, w_down.T, preferred_element_type=jnp.float32)
    d_gate = d_hidden * up_rows * gate_sig * (1.0 + gate * (1.0 - gate_sig))
    d_up = d_hidden * gate * gate_sig
    d_gate_up = jnp.concatenate([d_gate, d_up], axis=1).astype(jnp.bfloat16)
    g_gate_up = jnp.dot(c_low.T, d_gate_up, preferred_element_type=jnp.float32)
    d_two = jnp.dot(d_gate_up, w_gate_up.T, preferred_element_type=jnp.float32)
    d_norm_two, g_gain_two, g_bias_two = norm_backward(d_two, normed_two, scale_two, vectors[2])
    d_mid = d_rows + d_norm_two
    g_scale_attn = jnp.sum(d_mid * branch_attn, axis=0)
    d_branch = (d_mid * vectors[4]).astype(jnp.bfloat16)
    g_out = jnp.dot(attn_low.T, d_branch, preferred_element_type=jnp.float32)
    d_attn_low = jnp.dot(d_branch, w_out.T, preferred_element_type=jnp.float32).astype(jnp.bfloat16)
    d_attn = jnp.where(
        keep_rows[:, :, None, None],
        d_attn_low.reshape(seq_count, frame_span, head_count, head_size),
        jnp.zeros((), jnp.bfloat16),
    )
    seq_index = 0
    query_parts = []
    key_parts = []
    value_parts = []
    for number, head_start in enumerate(range(0, head_count, group_size)):
        head_end = head_start + group_size
        d_query, d_keys, d_values = attend_back(
            query_low[seq_index, :, head_start:head_end],
            key_wide[seq_index, :, head_start:head_end],
            value_wide[seq_index, :, head_start:head_end],
            window_mask[seq_index],
            total_list[seq_index][number],
            d_attn[seq_index, :, head_start:head_end],
        )
        query_parts.append(d_query)
        key_parts.append(d_keys)
        value_parts.append(d_values)
    query_grads = [jnp.concatenate(query_parts, axis=1)]
    key_grads = [jnp.concatenate(key_parts, axis=1)]
    value_grads = [jnp.concatenate(value_parts, axis=1)]
    d_query_all = jnp.stack(query_grads)
    d_pair = jnp.concatenate([jnp.stack(key_grads), jnp.stack(value_grads)], axis=2).reshape(
        seq_count, key_count, 2 * model_width
    )
    rim_rows = jnp.concatenate(
        [d_pair[:, :window_reach], d_pair[:, window_reach + frame_span :]], axis=1
    )
    taken_rows = padded(rim_rows.astype(jnp.bfloat16), (("seq", 1),), window_reach).astype(
        rim_rows.dtype
    )
    own_rows = d_pair[:, window_reach : window_reach + frame_span]
    own_rows = own_rows + jnp.pad(
        taken_rows[:, :window_reach], ((0, 0), (0, frame_span - window_reach), (0, 0))
    )
    own_rows = own_rows + jnp.pad(
        taken_rows[:, 3 * window_reach :], ((0, 0), (frame_span - window_reach, 0), (0, 0))
    )
    own_rows = own_rows.reshape(seq_count, frame_span, 2, head_count, head_size)
    d_qkv = jnp.stack(
        [
            rotate(d_query_all, pos_rows, -1.0),
            rotate(own_rows[:, :, 0], pos_rows, -1.0),
            own_rows[:, :, 1],
        ],
        axis=2,
    )
    d_qkv = d_qkv.reshape(row_count, 3 * model_width).astype(jnp.bfloat16)
    g_qkv = jnp.dot(a_low.T, d_qkv, preferred_element_type=jnp.float32)
    d_one = jnp.dot(d_qkv, w_qkv.T, preferred_element_type=jnp.float32)
    d_norm_one, g_gain_one, g_bias_one = norm_backward(d_one, normed_one, scale_one, vectors[0])
    frames_grad = (
        (d_mid + d_norm_one).astype(jnp.bfloat16).reshape(seq_count, frame_span, model_width)
    )
    small_grads = jnp.stack(
        [g_gain_one, g_bias_one, g_gain_two, g_bias_two, g_scale_attn, g_scale_mlp]
    )
    whole_grad = jnp.concatenate(
        [
            g_qkv.reshape(-1),
            g_out.reshape(-1),
            g_gate_up.reshape(-1),
            g_down.reshape(-1),
            small_grads.reshape(-1),
        ]
    )
    params_grad = lax.psum_scatter(whole_grad, ("dp", "seq"), scatter_dimension=0, tiled=True)
    new_params, new_first, new_second = adam_update(
        params, params_grad, first_moment, second_moment
    )
    return (output, frames_grad, params_grad, new_params, new_first, new_second)


EVERY = ("z", "x", "c", "y")
GROUP = ("z", "x")
RING = ((0, 0), (1, 0), (2, 0), (3, 0), (3, 1), (2, 1), (1, 1), (0, 1))
PLACES = tuple(2 * z + x for z, x in RING)
AHEAD = tuple((PLACES[i], PLACES[(i + 1) % 8]) for i in range(8))
BACK = tuple((b, a) for a, b in AHEAD)
SWAP = ((0, 1), (1, 0))
LINES = 4096
TAIL = 64
PITCH = 72
SLAB = 16
ROWS = 128 + SLAB
OWN = 256
SCALE = HEAD_DIM ** (-0.5)
SCALAR = pl.BlockSpec(memory_space=pltpu.SMEM)
WHOLE = pl.BlockSpec(memory_space=pltpu.VMEM)
HBM = pl.BlockSpec(memory_space=pltpu.HBM)
ANY = pl.BlockSpec(memory_space=pl.ANY)


def vmem(mebibytes):
    return pltpu.CompilerParams(vmem_limit_bytes=mebibytes << 20)


def ring_place(me, step):
    z, x = lax.div(me, 8), lax.rem(lax.div(me, 4), 2)
    at = lax.rem(jnp.where(x == 0, z, 7 - z) + step, 8)
    return jnp.where(at < 4, 2 * at, 15 - 2 * at)


def kind_of(shard):
    if shard < 6:
        return 0
    return 2 if 8 <= shard < 24 else 1


def piece_lines(kind, dest, pitch=64):
    place, member = divmod(dest, 4)
    if kind == 0:
        return [(512 * place + member, 8), (512 * place + 4 + member, 8)]
    if kind == 1:
        return [(1024 * member + place, 8), (1024 * member + 512 + place, 8)]
    return [(dest, pitch), (32 + dest, pitch)]


def tail_lines(kind, dest):
    place, member = divmod(dest, 4)
    if kind == 0:
        return [(0, 6, member, 8), (8, 6, 4 + member, 8)] if place == 0 else []
    if kind == 1:
        return [(0, 6, place, 8)] if member == 0 else []
    return [(0, 1, dest, 1)] + ([(8, 1, 32 + dest, 1)] if dest < 16 else [])


def is_kind(shard, kind):
    if kind == 0:
        return shard < 6
    gate_up = (shard >= 8) & (shard < 24)
    if kind == 2:
        return gate_up
    return (shard >= 6) & jnp.logical_not(gate_up) & (shard < 32)


def spread_kernel(me_ref, flat_ref, out_ref, lines_ref, tail_ref):
    me = me_ref[0]
    odd = lax.rem(me, 2) == 1
    start = 48 - (3 * me + 1) // 2
    lane = lax.broadcasted_iota(jnp.int32, (64, 128), 1)

    def shifted(step):
        here = flat_ref[pl.ds(start + step * 64, 64), :]
        after = flat_ref[pl.ds(start + step * 64 + 1, 64), :]
        mixed = jnp.where(lane < 64, pltpu.roll(here, 64, 1), pltpu.roll(after, 64, 1))
        return jnp.where(odd, mixed, here)

    def fill(pitch):
        def body(step, carry):
            lines_ref[pl.ds(pl.multiple_of(step * pitch, 8), 64), :] = shifted(step)
            return carry

        lax.fori_loop(0, LINES // 64, body, 0, unroll=4)

    tail_ref[...] = shifted(LINES // 64)
    for kind in range(3):

        @pl.when(is_kind(me, kind))
        def _(kind=kind):
            pitch = PITCH if kind == 2 else 64
            fill(pitch)
            for dest in range(32):
                for half, (first, stride) in enumerate(piece_lines(kind, dest, pitch)):
                    rows = lines_ref[pl.ds(first, 64, stride), :]
                    out_ref[dest, 64 * half : 64 * half + 64, :] = rows.astype(jnp.bfloat16)

    def slab_of(parts):
        slab = [jnp.zeros((8, 128), jnp.float32)] * 2
        row = lax.broadcasted_iota(jnp.int32, (8, 128), 0)
        for at, count, first, stride in parts:
            if count == 1:
                value = jnp.broadcast_to(tail_ref[first : first + 1, :], (8, 128))
            else:
                value = tail_ref[pl.ds(first, 8, stride), :]
            slab[at // 8] = jnp.where(row < count, value, 0.0)
        return jnp.concatenate(slab, axis=0).astype(jnp.bfloat16)

    for kind in range(3):

        @pl.when(is_kind(me + 1, kind))
        def _(kind=kind):
            for dest in range(32):
                out_ref[dest, 128:ROWS, :] = slab_of(tail_lines(kind, dest))

    @pl.when(me == 31)
    def _():
        for dest in range(32):
            out_ref[dest, 128:ROWS, :] = slab_of([(0, 6, 6 * (dest // 4), 1)])


def spread(params, me):
    flat = jnp.pad(params, (48 * 128, 4224 * 128 - 48 * 128 - params.shape[0])).reshape(4224, 128)
    return pl.pallas_call(
        spread_kernel,
        out_shape=jax.ShapeDtypeStruct((32, ROWS, 128), jnp.bfloat16),
        in_specs=[
            pl.BlockSpec(memory_space=pltpu.SMEM),
            pl.BlockSpec(memory_space=pltpu.VMEM),
        ],
        out_specs=pl.BlockSpec(memory_space=pltpu.VMEM),
        scratch_shapes=[
            pltpu.VMEM((LINES // 64 * PITCH, 128), jnp.float32),
            pltpu.VMEM((TAIL, 128), jnp.float32),
        ],
        compiler_params=vmem(12),
        name="spread",
    )(me, flat)


def collect_kernel(me_ref, piece_ref, out_ref, lines_ref, rows_ref):
    me = me_ref[0]
    odd = lax.rem(me, 2) == 1
    lines_ref[LINES:, :] = jnp.zeros((TAIL, 128), jnp.float32)
    for kind in range(3):

        @pl.when(is_kind(me, kind))
        def _(kind=kind):
            if kind == 2:
                for dest in range(32):
                    rows_ref[136 * dest : 136 * dest + 128, :] = piece_ref[dest, :128, :].astype(jnp.float32)
                for row in range(128):
                    first = 64 * (row % 64) + 32 * (row // 64)
                    lines_ref[first : first + 32, :] = rows_ref[pl.ds(row, 32, 136), :]
                return
            for dest in range(32):
                for half, (first, stride) in enumerate(piece_lines(kind, dest)):
                    rows = piece_ref[dest, 64 * half : 64 * half + 64, :].astype(jnp.float32)
                    lines_ref[pl.ds(first, 64, stride), :] = rows

    for kind in range(3):

        @pl.when(is_kind(me + 1, kind))
        def _(kind=kind):
            for dest in range(32):
                slab = piece_ref[dest, 128:ROWS, :].astype(jnp.float32)
                for at, count, first, stride in tail_lines(kind, dest):
                    for k in range(count):
                        line = LINES + first + k * stride
                        lines_ref[line : line + 1, :] = slab[at + k : at + k + 1, :]

    @pl.when(me == 31)
    def _():
        for place in range(8):
            total = piece_ref[4 * place, 128:ROWS, :].astype(jnp.float32)
            for member in range(1, 4):
                total = total + piece_ref[4 * place + member, 128:ROWS, :].astype(jnp.float32)
            for k in range(6):
                line = LINES + 6 * place + k
                lines_ref[line : line + 1, :] = total[k : k + 1, :]

    start = (3 * me) // 2
    lane = lax.broadcasted_iota(jnp.int32, (24, 128), 1)

    def shift(step, carry):
        here = lines_ref[pl.ds(start + step * 24, 24), :]
        after = lines_ref[pl.ds(start + step * 24 + 1, 24), :]
        mixed = jnp.where(lane < 64, pltpu.roll(here, 64, 1), pltpu.roll(after, 64, 1))
        out_ref[pl.ds(pl.multiple_of(step * 24, 8), 24), :] = jnp.where(odd, mixed, here)
        return carry

    lax.fori_loop(0, 4104 // 24, shift, 0, unroll=9)


def collect(pieces, me, count):
    lines = pl.pallas_call(
        collect_kernel,
        out_shape=jax.ShapeDtypeStruct((4104, 128), jnp.float32),
        in_specs=[
            pl.BlockSpec(memory_space=pltpu.SMEM),
            pl.BlockSpec(memory_space=pltpu.VMEM),
        ],
        out_specs=pl.BlockSpec(memory_space=pltpu.VMEM),
        scratch_shapes=[
            pltpu.VMEM((LINES + TAIL, 128), jnp.float32),
            pltpu.VMEM((32 * 136, 128), jnp.float32),
        ],
        compiler_params=vmem(12),
        name="collect",
    )(me, pieces)
    return lines.reshape(-1)[:count]


def swap_halves(rows):
    lane = lax.broadcasted_iota(jnp.int32, rows.shape, 1)
    return jnp.where(
        lax.rem(lane, 64) < 32, pltpu.roll(rows, 96, 1), pltpu.roll(rows, 32, 1)
    )


def turn(rows, cosine, signed_sine):
    parts = []
    for at in range(0, rows.shape[1], 128):
        part = rows[:, at : at + 128]
        parts.append(part * cosine + swap_halves(part) * signed_sine)
    return jnp.concatenate(parts, axis=1)


def clip_of(length_ref, frame):
    first = length_ref[0, 0]
    return (frame >= first).astype(jnp.int32) + (frame >= first + length_ref[0, 1]).astype(jnp.int32)


def mask_of(length_ref, block):
    row = lax.broadcasted_iota(jnp.int32, (256, 384), 0) + 256 * block
    key = lax.broadcasted_iota(jnp.int32, (256, 384), 1) + 128 * block
    own = clip_of(length_ref, lax.broadcasted_iota(jnp.int32, (256, 1), 0) + 256 * block)
    others = clip_of(length_ref, lax.broadcasted_iota(jnp.int32, (1, 384), 1) + 128 * block)
    return (jnp.abs(row - key) < WINDOW) & (own == others), own != 1


def nt(left, right):
    return lax.dot_general(left, right, (((1,), (1,)), ((), ())), preferred_element_type=jnp.float32)


def tn(left, right):
    return lax.dot_general(left, right, (((0,), (0,)), ((), ())), preferred_element_type=jnp.float32)


def nn(left, right):
    return jnp.dot(left, right, preferred_element_type=jnp.float32)


def cost(flops, moved):
    return pl.CostEstimate(flops=flops, bytes_accessed=moved, transcendentals=0)


def fix_kernel(piece_ref, first_ref, second_ref, third_ref):
    for source in range(32):
        out, at = (first_ref, source) if source < 8 else (second_ref, source - 8) if source < 24 else (third_ref, source - 24)
        out[128 * at : 128 * at + 128, :] = piece_ref[source, :128, :]
        if source:
            slab = piece_ref[source - 1, 128:ROWS, :].astype(jnp.float32)
            for half in range(2):
                rows = piece_ref[source, 64 * half : 64 * half + 16, :].astype(jnp.float32)
                extra = jnp.concatenate([slab[8 * half : 8 * half + 8], jnp.zeros((8, 128), jnp.float32)])
                out[128 * at + 64 * half : 128 * at + 64 * half + 16, :] = (rows + extra).astype(jnp.bfloat16)
    first_ref[1024:, :] = piece_ref[31, 128:ROWS, :]


def fix(pieces):
    return pl.pallas_call(
        fix_kernel,
        out_shape=tuple(jax.ShapeDtypeStruct((n, 128), jnp.bfloat16) for n in (1024 + SLAB, 2048, 1024)),
        in_specs=[WHOLE],
        out_specs=(WHOLE,) * 3,
        compiler_params=vmem(12),
        cost_estimate=cost(0, 1 << 22),
        name="fix",
    )(pieces)


def in_order(refs, seq, half, second):
    mine, other = refs[2 * seq], refs[2 * seq + 1]
    return jnp.where(lax.rem(second, 2) == half, mine[...], other[...])


def ring_parts(me_ref, refs):
    me = me_ref[0]
    parts = [(ring_place(me, 0), refs[0], None)]
    for step in range(1, 4):
        parts += [(ring_place(me, 8 - step), refs[2 * step - 1], None), (ring_place(me, step), refs[2 * step], None)]
    half = refs[7].shape[0]
    last = ring_place(me, 4)
    return parts + [(last, refs[7], (0, half)), (last, refs[8], (half, half + refs[8].shape[0]))]


def copy_all(pairs, done):
    copies = [pltpu.make_async_copy(source, target, done.at[k]) for k, (source, target) in enumerate(pairs)]
    for copy in copies:
        copy.start()
    for copy in copies:
        copy.wait()


def join_first_kernel(me_ref, *refs):
    blocks, (qkv_ref, out_ref, vec_ref, lines_ref, _) = refs[:9], refs[9:]
    for place, block, rows in ring_parts(me_ref, blocks):
        lo, hi = rows or (0, 1024 + SLAB)
        for at, end, ref in ((0, 768, qkv_ref), (768, 1024, out_ref), (1024, 1024 + SLAB, lines_ref)):
            first, last = max(at, lo), min(end, hi)
            if first < last:
                ref[place, first - at : last - at, :] = block[first - lo : last - lo, :]
    slabs = [lines_ref[place].astype(jnp.float32) for place in range(8)]
    for v in range(6):
        for k in range(8):
            line = 8 * v + k
            vec_ref[v : v + 1, 128 * k : 128 * k + 128] = slabs[line // 6][line % 6 : line % 6 + 1]


def join_gate_up_kernel(which, me_ref, *refs):
    blocks, (out_ref, done) = refs[:9], refs[-2:]
    pairs = []
    for place, block, rows in ring_parts(me_ref, blocks)[which]:
        lo, hi = rows or (0, 16)
        for half in range(2):
            at = pl.multiple_of(256 * half + 128 * lax.rem(place, 2), 128)
            pairs.append((block.at[:, half], out_ref.at[lax.div(place, 2), lo:hi, :, pl.ds(at, 128)]))
    copy_all(pairs, done)


def join_down_kernel(which, me_ref, *refs):
    blocks, (out_ref, done) = refs[:9], refs[-2:]
    pairs = []
    for place, block, rows in ring_parts(me_ref, blocks)[which]:
        lo, hi = rows or (0, 1024)
        pairs.append((block, out_ref.at[lo:hi, pl.ds(pl.multiple_of(128 * place, 128), 128)]))
    copy_all(pairs, done)


def join_out_kernel(*refs):
    w_ref = refs[4]
    for k in range(4):
        for place in range(8):
            w_ref[256 * k : 256 * k + 256, 128 * place : 128 * place + 128] = refs[k][place]


def join_out(parts):
    return pl.pallas_call(
        join_out_kernel,
        out_shape=jax.ShapeDtypeStruct((D, D), jnp.bfloat16),
        in_specs=[WHOLE] * 4,
        out_specs=WHOLE,
        compiler_params=vmem(12),
        cost_estimate=cost(0, 4 << 20),
        name="join_out",
    )(*parts)


def join(kernel, me, blocks, out_shape, name, scratch=(), space=WHOLE):
    if space is HBM:
        blocks = [pltpu.with_memory_space_constraint(block, pltpu.HBM) for block in blocks]
    return pl.pallas_call(
        kernel,
        out_shape=out_shape,
        in_specs=[SCALAR] + [space] * 9,
        out_specs=jax.tree.map(lambda _: WHOLE, out_shape),
        scratch_shapes=list(scratch) + [pltpu.SemaphoreType.DMA((32,))],
        compiler_params=vmem(12),
        cost_estimate=cost(0, 4 << 20),
        name=name,
    )(me, *blocks)


def join_rest_kernel(kernel, me_ref, last_ref, end_ref, _, out_ref, done):
    kernel(slice(7, 9), me_ref, *([last_ref] * 8 + [end_ref]), out_ref, done)


def join_twice(kernel, me, blocks, out_shape, name):
    early = [pltpu.with_memory_space_constraint(block, pltpu.HBM) for block in blocks[:7]]
    whole = pl.pallas_call(
        lambda me_ref, *refs: kernel(slice(0, 7), me_ref, *refs[:7], refs[6], refs[6], *refs[7:]),
        out_shape=out_shape,
        in_specs=[SCALAR] + [HBM] * 7,
        out_specs=WHOLE,
        scratch_shapes=[pltpu.SemaphoreType.DMA((32,))],
        compiler_params=vmem(12),
        cost_estimate=cost(0, 4 << 20),
        name=name,
    )(me, *early)
    last = after(tuple(blocks[7:]), whole)
    return pl.pallas_call(
        functools.partial(join_rest_kernel, kernel),
        out_shape=out_shape,
        in_specs=[SCALAR, ANY, ANY, WHOLE],
        out_specs=WHOLE,
        input_output_aliases={3: 0},
        scratch_shapes=[pltpu.SemaphoreType.DMA((32,))],
        compiler_params=vmem(12),
        cost_estimate=cost(0, 4 << 20),
        name=name + "_rest",
    )(me, *last, whole)


def prep_kernel(y_ref, own_ref, pair_ref, far_ref, last_ref, x_ref, mean_ref, inv_ref):
    for block in range(4):
        rows = slice(256 * block, 256 * block + 256)
        x_low = in_order((own_ref, pair_ref, far_ref, last_ref), block // 2, block % 2, y_ref[0])
        x_ref[rows, :] = x_low
        x_rows = x_low.astype(jnp.float32)
        mean = jnp.mean(x_rows, axis=1, keepdims=True)
        centered = x_rows - mean
        mean_ref[rows, :] = mean
        inv_ref[rows, :] = lax.rsqrt(jnp.mean(centered * centered, axis=1, keepdims=True) + eps_norm)


def prep(second, rows):
    return pl.pallas_call(
        prep_kernel,
        out_shape=(
            jax.ShapeDtypeStruct((1024, D), jnp.bfloat16),
            jax.ShapeDtypeStruct((1024, 1), jnp.float32),
            jax.ShapeDtypeStruct((1024, 1), jnp.float32),
        ),
        in_specs=[SCALAR] + [WHOLE] * 4,
        out_specs=(WHOLE,) * 3,
        compiler_params=vmem(12),
        cost_estimate=cost(1 << 24, 5 << 20),
        name="prep",
    )(second, *rows)


def front_kernel(
    x_ref, mean_ref, inv_ref, ring_ref, vec_ref, order_ref, cos_ref, sin_ref, length_ref, far_length_ref,
    a_out, w_out, low_out, attn_ref, lse_out,
    a_ref, w_ref, low_ref, lse_ref, done,
):
    copies = [
        pltpu.make_async_copy(ref, out, done.at[k])
        for k, (ref, out) in enumerate(((w_ref, w_out), (a_ref, a_out), (low_ref, low_out), (lse_ref, lse_out)))
    ]
    gain, bias = vec_ref[0:1, :], vec_ref[1:2, :]
    for block in range(8):
        parts = []
        for chunk in range(6 * block, 6 * block + 6):
            at = 128 * (chunk // 8)
            parts.append(
                jnp.concatenate(
                    [ring_ref[chunk % 8, at : at + 64, :], ring_ref[chunk % 8, at + 64 : at + 128, :]], axis=1
                )
            )
        rows = nn(order_ref[...], jnp.concatenate(parts, axis=0)).astype(jnp.bfloat16)
        for third in range(3):
            w_ref[128 * block : 128 * block + 128, OWN * third : OWN * third + OWN] = rows[
                128 * third : 128 * third + 128
            ]
    copies[0].start()
    for block in range(4):
        rows = slice(256 * block, 256 * block + 256)
        seq, at = block // 2, 256 * (block % 2)
        normed = (x_ref[rows, :].astype(jnp.float32) - mean_ref[rows, :]) * inv_ref[rows, :]
        a_low = (normed * gain + bias).astype(jnp.bfloat16)
        a_ref[rows, :] = a_low
        qkv = nn(a_low, w_ref[...])
        cosine, sine = cos_ref[seq, at : at + 256, :], sin_ref[seq, at : at + 256, :]
        low_ref[rows, : 2 * OWN] = turn(qkv[:, : 2 * OWN], cosine, sine).astype(jnp.bfloat16)
        low_ref[rows, 2 * OWN :] = qkv[:, 2 * OWN :].astype(jnp.bfloat16)
    copies[1].start()
    copies[2].start()
    for seq in range(2):
        for block in range(2):
            at = 512 * seq + 256 * block
            rows = slice(at, at + 256)
            keys = slice(512 * seq + 128 * block, 512 * seq + 128 * block + 384)
            mask, keep = mask_of((length_ref, far_length_ref)[seq], block)
            heads, sums = [], []
            for head in range(4):
                lane = 64 * head
                query = low_ref[rows, lane : lane + 64]
                key = low_ref[keys, OWN + lane : OWN + lane + 64]
                value = low_ref[keys, 2 * OWN + lane : 2 * OWN + lane + 64]
                masked = jnp.where(mask, nt(query, key) * SCALE, neg_large)
                top = jnp.max(masked, axis=1, keepdims=True)
                weight = jnp.exp(masked - top)
                total = jnp.sum(weight, axis=1, keepdims=True)
                probs = (weight * (1.0 / total)).astype(jnp.bfloat16)
                heads.append(jnp.where(keep, nn(probs, value), 0.0))
                sums.append(top + jnp.log(total))
            attn_ref[rows, :] = jnp.concatenate(heads, axis=1).astype(jnp.bfloat16)
            lse_ref[rows, :] = jnp.concatenate(sums, axis=1)
    copies[3].start()
    for copy in copies:
        copy.wait()


def front(x_all, mean, inv, ring, vectors, order, cosine, sine, lengths):
    return pl.pallas_call(
        front_kernel,
        out_shape=(
            pltpu.HBM((1024, D), jnp.bfloat16),
            pltpu.HBM((D, 3 * OWN), jnp.bfloat16),
            pltpu.HBM((1024, 3 * OWN), jnp.bfloat16),
            jax.ShapeDtypeStruct((1024, OWN), jnp.bfloat16),
            pltpu.HBM((1024, 4), jnp.float32),
        ),
        in_specs=[WHOLE] * 8 + [SCALAR] * 2,
        out_specs=(HBM, HBM, HBM, WHOLE, HBM),
        scratch_shapes=[
            pltpu.VMEM((1024, D), jnp.bfloat16),
            pltpu.VMEM((D, 3 * OWN), jnp.bfloat16),
            pltpu.VMEM((1024, 3 * OWN), jnp.bfloat16),
            pltpu.VMEM((1024, 4), jnp.float32),
            pltpu.SemaphoreType.DMA((4,)),
        ],
        compiler_params=vmem(14),
        cost_estimate=cost(12 << 30, 8 << 20),
        name="front",
    )(x_all, mean, inv, ring, vectors, order, cosine, sine, *lengths)


def mix_kernel(x_ref, own_ref, pair_ref, far_ref, last_ref, w_ref, vec_ref, c_ref, branch_ref):
    for block in range(4):
        rows = slice(256 * block, 256 * block + 256)
        other = (block + 2) % 4
        far = slice(256 * other, 256 * other + 256)
        attn = jnp.concatenate([own_ref[rows, :], pair_ref[rows, :], far_ref[far, :], last_ref[far, :]], axis=1)
        branch = nn(attn, w_ref[...])
        normed, _ = normed_of(x_ref[rows, :].astype(jnp.float32) + vec_ref[4:5, :] * branch)
        c_ref[rows, :] = (normed * vec_ref[2:3, :] + vec_ref[3:4, :]).astype(jnp.bfloat16)
        if block < 2:
            branch_ref[rows, :] = branch


def mix(x_all, attn, w_out, vectors):
    return pl.pallas_call(
        mix_kernel,
        out_shape=(
            pltpu.VMEM((1024, D), jnp.bfloat16),
            jax.ShapeDtypeStruct((512, D), jnp.float32),
        ),
        in_specs=[WHOLE] * 7,
        out_specs=(WHOLE, WHOLE),
        compiler_params=vmem(12),
        cost_estimate=cost(3 << 30, 10 << 20),
        name="mix",
    )(x_all, *attn, w_out, vectors)


def gate_kernel(c_ref, w_ref, gate_up_ref, hidden_ref):
    for block in range(4):
        rows = slice(256 * block, 256 * block + 256)
        for chunk in range(4):
            both = nn(c_ref[rows, :], w_ref[chunk])
            gate_up_ref[chunk, rows, :] = both
            gate, up = both[:, :256], both[:, 256:]
            hidden_ref[rows, 256 * chunk : 256 * chunk + 256] = (gate * jax.nn.sigmoid(gate) * up).astype(
                jnp.bfloat16
            )


def gate_step(c_low, w_gate_up):
    return pl.pallas_call(
        gate_kernel,
        out_shape=(
            jax.ShapeDtypeStruct((4, 1024, 512), jnp.float32),
            jax.ShapeDtypeStruct((1024, 1024), jnp.bfloat16),
        ),
        in_specs=[WHOLE] * 2,
        out_specs=(WHOLE, WHOLE),
        compiler_params=vmem(12),
        cost_estimate=cost(5 << 30, 16 << 20),
        name="gate",
    )(c_low, w_gate_up)


def down_grad_kernel(me_ref, hidden_ref, own_ref, pair_ref, far_ref, last_ref, vec_ref, g_ref, d_mlp_ref):
    for block in range(4):
        rows = in_order((own_ref, pair_ref, far_ref, last_ref), block // 2, block % 2, me_ref[0])
        d_mlp_ref[256 * block : 256 * block + 256, :] = (rows.astype(jnp.float32) * vec_ref[5:6, :]).astype(
            jnp.bfloat16
        )
    for source in range(0, 8, 2):
        g_down = tn(hidden_ref[:, 128 * source : 128 * source + 256], d_mlp_ref[...]).astype(jnp.bfloat16)
        for pair in range(2):
            for place in range(8):
                at = 128 * (source + pair)
                g_ref[place, at : at + 128, :] = g_down[128 * pair : 128 * pair + 128, 128 * place : 128 * place + 128]


def down_grad(me, hidden, cot, vectors):
    return pl.pallas_call(
        down_grad_kernel,
        out_shape=(
            jax.ShapeDtypeStruct((8, 1024, 128), jnp.bfloat16),
            jax.ShapeDtypeStruct((1024, D), jnp.bfloat16),
        ),
        in_specs=[SCALAR] + [WHOLE] * 6,
        out_specs=(WHOLE, WHOLE),
        compiler_params=vmem(12),
        cost_estimate=cost(3 << 30, 8 << 20),
        name="down_grad",
    )(me, hidden, *cot, vectors)


def put_rows(me, whole_ref, refs, done=None):
    y = lax.rem(me, 2)
    copies = []
    for k, (ref, half) in enumerate(zip(refs, (1 - y, y, 1 - y, y))):
        rows = pl.ds(pl.multiple_of(512 * (k // 2) + 256 * half, 256), 256)
        if done is not None and k < 2:
            copies.append(pltpu.make_async_copy(whole_ref.at[rows, :], ref, done.at[k]))
            copies[-1].start()
        else:
            ref[...] = whole_ref[rows, :].astype(ref.dtype)
    for copy in copies:
        copy.wait()


PARTS = tuple(jax.ShapeDtypeStruct((256, D), t) for t in (jnp.float32, jnp.float32, jnp.bfloat16, jnp.bfloat16))


def hidden_back_kernel(gate_up_ref, d_mlp_ref, w_ref, d_both_ref):
    for block in range(4):
        rows = slice(256 * block, 256 * block + 256)
        for chunk in range(4):
            d_hidden = nt(d_mlp_ref[rows, :], w_ref[256 * chunk : 256 * chunk + 256, :])
            gate, up = gate_up_ref[chunk, rows, :256], gate_up_ref[chunk, rows, 256:]
            sig = jax.nn.sigmoid(gate)
            d_both_ref[chunk, rows, :256] = (d_hidden * up * sig * (1.0 + gate * (1.0 - sig))).astype(jnp.bfloat16)
            d_both_ref[chunk, rows, 256:] = (d_hidden * gate * sig).astype(jnp.bfloat16)


def hidden_back(gate_up, d_mlp, w_down):
    return pl.pallas_call(
        hidden_back_kernel,
        out_shape=jax.ShapeDtypeStruct((4, 1024, 512), jnp.bfloat16),
        in_specs=[WHOLE] * 3,
        out_specs=WHOLE,
        compiler_params=vmem(12),
        cost_estimate=cost(4 << 30, 18 << 20),
        name="hidden_back",
    )(gate_up, d_mlp, w_down)


def norm_back_kernel(y_ref, d_both_ref, w_ref, near_sent_ref, near_ref, far_sent_ref, far_ref, d_c_ref):
    for block in range(4):
        rows = slice(256 * block, 256 * block + 256)
        d_c = nt(d_both_ref[0, rows, :], w_ref[0])
        for chunk in range(1, 4):
            d_c += nt(d_both_ref[chunk, rows, :], w_ref[chunk])
        d_c_ref[rows, :] = d_c
    put_rows(y_ref[0], d_c_ref, (near_sent_ref, near_ref, far_sent_ref, far_ref))


def norm_back(second, d_both, w_gate_up):
    return pl.pallas_call(
        norm_back_kernel,
        out_shape=PARTS,
        in_specs=[SCALAR, WHOLE, WHOLE],
        scratch_shapes=[pltpu.VMEM((1024, D), jnp.float32)],
        out_specs=(WHOLE,) * 4,
        compiler_params=vmem(12),
        cost_estimate=cost(5 << 30, 12 << 20),
        name="norm_back",
    )(second, d_both, w_gate_up)


def gate_grad_kernel(c_ref, d_both_ref, g_ref):
    for chunk in range(4):
        for block in range(4):
            grad = tn(c_ref[:, 256 * block : 256 * block + 256], d_both_ref[chunk]).astype(jnp.bfloat16)
            for part in range(4):
                source = 4 * block + part
                for pair in range(2):
                    for half in range(2):
                        at = 256 * half + 128 * pair
                        first = 128 * source + 64 * half
                        g_ref[2 * chunk + pair, first : first + 64, :] = grad[64 * part : 64 * part + 64, at : at + 128]


def gate_grad(c_low, d_both):
    return pl.pallas_call(
        gate_grad_kernel,
        out_shape=jax.ShapeDtypeStruct((8, 2048, 128), jnp.bfloat16),
        in_specs=[WHOLE] * 2,
        out_specs=WHOLE,
        compiler_params=vmem(12),
        cost_estimate=cost(5 << 30, 10 << 20),
        name="gate_grad",
    )(c_low, d_both)


def out_kernel(
    y_ref, hidden_ref, w_ref, own_ref, pair_ref, last_ref, end_ref,
    near_sent_ref, near_ref, far_sent_ref, far_ref, g_scale_ref,
    branch_ref, done,
):
    total = jnp.zeros((1, D), jnp.float32)
    for block in range(4):
        rows = slice(256 * block, 256 * block + 256)
        branch = nn(hidden_ref[rows, :], w_ref[...])
        branch_ref[rows, :] = branch
        cot = in_order((own_ref, pair_ref, last_ref, end_ref), block // 2, block % 2, y_ref[0])
        total += jnp.sum(cot.astype(jnp.float32) * branch, axis=0, keepdims=True)
    g_scale_ref[...] = total
    put_rows(y_ref[0], branch_ref, (near_sent_ref, near_ref, far_sent_ref, far_ref), done)


def out_step(second, hidden, down, cot):
    return pl.pallas_call(
        out_kernel,
        out_shape=(pltpu.HBM((256, D), jnp.float32),) * 2 + PARTS[2:] + (jax.ShapeDtypeStruct((1, D), jnp.float32),),
        in_specs=[SCALAR] + [WHOLE] * 6,
        scratch_shapes=[pltpu.VMEM((1024, D), jnp.float32), pltpu.SemaphoreType.DMA((2,))],
        out_specs=(HBM, HBM, WHOLE, WHOLE, WHOLE),
        compiler_params=vmem(12),
        cost_estimate=cost(3 << 30, 10 << 20),
        name="out",
    )(second, hidden, down, *cot)


def attend_back_kernel(
    y_ref, own_ref, pair_ref, far_ref, last_ref, ring_ref, attn_ref, low_ref, lse_ref, cos_ref, sin_ref,
    length_ref, far_length_ref,
    d_qkv_ref, g_ref,
    d_branch_ref, w_out_ref, key_ref, value_ref,
):
    for place in range(8):
        w_out_ref[:, 128 * place : 128 * place + 128] = ring_ref[place]
    for block in range(4):
        d_branch_ref[256 * block : 256 * block + 256, :] = in_order(
            (own_ref, pair_ref, far_ref, last_ref), block // 2, block % 2, y_ref[0]
        )
    g_out = tn(attn_ref[...], d_branch_ref[...]).astype(jnp.bfloat16)
    for place in range(8):
        g_ref[place] = g_out[:, 128 * place : 128 * place + 128]
    for seq in range(2):
        key_ref[...] = jnp.zeros_like(key_ref)
        value_ref[...] = jnp.zeros_like(value_ref)
        cosine, sine = cos_ref[seq], -sin_ref[seq]
        for block in range(2):
            at = 512 * seq + 256 * block
            rows = slice(at, at + 256)
            span = slice(128 * block, 128 * block + 384)
            keys = slice(512 * seq + 128 * block, 512 * seq + 128 * block + 384)
            mask, keep = mask_of((length_ref, far_length_ref)[seq], block)
            d_attn_all = nt(d_branch_ref[rows, :], w_out_ref[...]).astype(jnp.bfloat16)
            d_attn_all = jnp.where(keep, d_attn_all, jnp.zeros_like(d_attn_all))
            d_queries, d_keys, d_values = [], [], []
            for head in range(4):
                lane = 64 * head
                query = low_ref[rows, lane : lane + 64]
                key = low_ref[keys, OWN + lane : OWN + lane + 64]
                value = low_ref[keys, 2 * OWN + lane : 2 * OWN + lane + 64]
                d_attn = d_attn_all[:, lane : lane + 64]
                masked = jnp.where(mask, nt(query, key) * SCALE, neg_large)
                probs = jnp.exp(masked - lse_ref[rows, head : head + 1])
                d_values.append(tn(probs.astype(jnp.bfloat16), d_attn))
                d_probs = nt(d_attn, value)
                inner = jnp.sum(probs * d_probs, axis=1, keepdims=True)
                d_scores = (probs * (d_probs - inner)).astype(jnp.bfloat16)
                d_queries.append(nn(d_scores, key) * SCALE)
                d_keys.append(tn(d_scores, query) * SCALE)
            part = slice(256 * block, 256 * block + 256)
            d_query = turn(jnp.concatenate(d_queries, axis=1), cosine[part], sine[part])
            d_qkv_ref[rows, :OWN] = d_query.astype(jnp.bfloat16)
            key_ref[span, :] += jnp.concatenate(d_keys, axis=1)
            value_ref[span, :] += jnp.concatenate(d_values, axis=1)
        whole = slice(512 * seq, 512 * seq + 512)
        d_qkv_ref[whole, OWN : 2 * OWN] = turn(key_ref[...], cosine, sine).astype(jnp.bfloat16)
        d_qkv_ref[whole, 2 * OWN :] = value_ref[...].astype(jnp.bfloat16)


def attention_back(me, d_branch, ring, attn, low, lse, cosine, sine, lengths):
    return pl.pallas_call(
        attend_back_kernel,
        out_shape=(
            jax.ShapeDtypeStruct((1024, 3 * OWN), jnp.bfloat16),
            jax.ShapeDtypeStruct((8, OWN, 128), jnp.bfloat16),
        ),
        in_specs=[SCALAR] + [WHOLE] * 10 + [SCALAR] * 2,
        out_specs=(WHOLE, WHOLE),
        scratch_shapes=[
            pltpu.VMEM((1024, D), jnp.bfloat16),
            pltpu.VMEM((OWN, D), jnp.bfloat16),
            pltpu.VMEM((512, OWN), jnp.float32),
            pltpu.VMEM((512, OWN), jnp.float32),
        ],
        compiler_params=vmem(12),
        cost_estimate=cost(12 << 30, 10 << 20),
        name="attend_back",
    )(me, *d_branch, ring, attn, low, lse, cosine, sine, *lengths)


def grad_kernel(
    y_ref, a_ref, w_ref, order_ref, d_qkv_ref, g_out_ref, x_ref, mean_ref, inv_ref, small_ref,
    g_ref, near_sent_ref, near_ref, far_sent_ref, far_ref,
    d_a_ref,
):
    g_gain, g_bias = jnp.zeros((1, D), jnp.float32), jnp.zeros((1, D), jnp.float32)
    for block in range(4):
        rows = slice(256 * block, 256 * block + 256)
        d_a = nt(d_qkv_ref[rows, :], w_ref[...])
        normed = (x_ref[rows, :].astype(jnp.float32) - mean_ref[rows, :]) * inv_ref[rows, :]
        g_gain += jnp.sum(d_a * normed, axis=0, keepdims=True)
        g_bias += jnp.sum(d_a, axis=0, keepdims=True)
        d_a_ref[rows, :] = d_a
    put_rows(y_ref[0], d_a_ref, (near_sent_ref, near_ref, far_sent_ref, far_ref))
    for block in range(8):
        grad = tn(a_ref[:, 128 * block : 128 * block + 128], d_qkv_ref[...]).astype(jnp.bfloat16)
        grad = jnp.concatenate([grad[:, OWN * third : OWN * third + OWN] for third in range(3)], axis=0)
        grad = tn(order_ref[...], grad).astype(jnp.bfloat16)
        for part in range(6):
            chunk = 6 * block + part
            at = 128 * (chunk // 8)
            g_ref[chunk % 8, at : at + 64, :] = grad[64 * part : 64 * part + 64, :128]
            g_ref[chunk % 8, at + 64 : at + 128, :] = grad[64 * part : 64 * part + 64, 128:]
    vectors = [g_gain, g_bias] + [small_ref[k : k + 1, :] for k in range(4)]
    lines = [v[:, 128 * k : 128 * k + 128] for v in vectors for k in range(8)]
    for place in range(8):
        g_ref[place, 768:1024, :] = g_out_ref[place]
        rows = lines[6 * place : 6 * place + 6] + [jnp.zeros((SLAB - 6, 128), jnp.float32)]
        g_ref[place, 1024:, :] = jnp.concatenate(rows, axis=0).astype(jnp.bfloat16)


def grad_step(second, a_low, w_qkv, order, d_qkv, g_out, x_all, mean, inv, small):
    return pl.pallas_call(
        grad_kernel,
        out_shape=(jax.ShapeDtypeStruct((8, 1024 + SLAB, 128), jnp.bfloat16),) + PARTS,
        in_specs=[SCALAR] + [WHOLE] * 9,
        scratch_shapes=[pltpu.VMEM((1024, D), jnp.float32)],
        out_specs=(WHOLE,) * 5,
        compiler_params=vmem(12),
        cost_estimate=cost(8 << 30, 12 << 20),
        name="grad",
    )(second, a_low, w_qkv, order, d_qkv, g_out, x_all, mean, inv, small)


def after(values, *others):
    if isinstance(values, tuple):
        return lax.optimization_barrier(values + others)[: len(values)]
    return lax.optimization_barrier((values,) + others)[0]


def both_ways(ahead, back):
    return lax.optimization_barrier((lax.ppermute(ahead, GROUP, AHEAD), lax.ppermute(back, GROUP, BACK)))


class Gather:
    def __init__(self, block):
        self.blocks = [block]
        self.next = (block, block)
        self.half = (block.shape[0] // 2 + 15) // 16 * 16
        self.count = 0

    def step(self, *waits, hold=()):
        self.count += 1
        ahead, back = after(self.next, *waits) if waits else self.next
        if self.count == 4:
            ahead, back = ahead[: self.half], back[self.half :]
        self.next = after(both_ways(ahead, back), *hold)
        self.blocks += self.next
        return self.next


class Scatter:
    def __init__(self, blocks, me):
        self.blocks, self.me = blocks, me
        self.rows = blocks.shape[1]
        self.half = (self.rows // 2 + 15) // 16 * 16
        self.count = 0
        self.next = (self.get(4, 0, self.half), self.get(4, self.half))

    def get(self, step, lo=0, hi=None):
        hi = self.rows if hi is None else hi
        at = (ring_place(self.me, step % 8), 0 * self.me + lo, 0 * self.me)
        return lax.dynamic_slice(self.blocks, at, (1, hi - lo, 128))[0]

    def step(self, *waits, hold=()):
        self.count += 1
        ahead, back = came = after(both_ways(*(after(self.next, *waits) if waits else self.next)), *hold)

        def add(moved, own):
            return (moved.astype(jnp.float32) + own.astype(jnp.float32)).astype(jnp.bfloat16)

        if self.count == 1:
            half = self.half
            ahead = jnp.concatenate([add(ahead, self.get(3, 0, half)), self.get(3, half)])
            back = jnp.concatenate([self.get(5, 0, half), add(back, self.get(5, half))])
        elif self.count < 4:
            ahead, back = add(ahead, self.get(4 - self.count)), add(back, self.get(4 + self.count))
        else:
            total = self.get(0).astype(jnp.float32) + ahead.astype(jnp.float32) + back.astype(jnp.float32)
            self.total = total.astype(jnp.bfloat16)
        self.next = (ahead, back)
        return came


def to_pair(rows, *waits):
    rows = after(rows, *waits) if waits else rows
    return rows, lax.ppermute(rows, "y", SWAP)


def to_group(pair, *waits):
    pair = after(tuple(pair), *waits) if waits else pair
    return tuple(pair) + tuple(lax.ppermute(rows, "c", SWAP) for rows in pair)


def half_sum(near_sent, near, far_sent, far):
    sent = near_sent + lax.ppermute(far_sent, "c", SWAP).astype(jnp.float32)
    kept = near + lax.ppermute(far, "c", SWAP).astype(jnp.float32)
    return lax.optimization_barrier((sent.astype(jnp.bfloat16), kept))


def full_sum(sent, kept):
    return kept + lax.ppermute(sent, "y", SWAP).astype(jnp.float32)


def normed_of(rows):
    centered = rows - jnp.mean(rows, axis=-1, keepdims=True)
    inv_scale = lax.rsqrt(jnp.mean(centered * centered, axis=-1, keepdims=True) + eps_norm)
    return centered * inv_scale, inv_scale


def norm_rows_back(out_grad, normed, inv_scale, gain):
    inner = out_grad * gain
    return inv_scale * (
        inner
        - jnp.mean(inner, axis=-1, keepdims=True)
        - normed * jnp.mean(inner * normed, axis=-1, keepdims=True)
    )


def fast_body(frames, cotangent, clip_lengths, params, first_moment, second_moment):
    z, x, c, y = (lax.axis_index(axis) for axis in EVERY)
    device = (((z * 2 + x) * 2 + c) * 2 + y).astype(jnp.int32)
    me = device[None]
    lengths = (clip_lengths, lax.ppermute(clip_lengths, "c", SWAP))
    order = np.zeros((384, 384), np.float32)
    for row in range(384):
        order[(row % 3) * 128 + row // 3, row] = 1.0
    order = jnp.asarray(order, jnp.bfloat16)

    pieces = spread(params, me)
    pieces = lax.all_to_all(pieces, EVERY, split_axis=0, concat_axis=0, tiled=True)
    first_piece, second_piece, third_piece = fix(pieces)
    first, second, third = Gather(first_piece), Gather(second_piece), Gather(third_piece)
    frames_pair = to_pair(frames[0], first_piece)
    came = first.step()
    cot_pair = to_pair(cotangent[0], frames_pair[1])
    lengths = after(lengths, first_piece)
    both = jnp.concatenate(lengths)
    frame = jnp.arange(512, dtype=jnp.int32)
    starts, ends = both[:, :1], both[:, :1] + both[:, 1:]
    position = jnp.where((frame >= starts) & (frame < ends), frame - starts, frame).astype(jnp.float32)
    inverse = jnp.exp(
        jnp.asarray(np.arange(128) % 32, jnp.float32) * (-2.0 * math.log(rope_base) / HEAD_DIM)
    )
    angle = position[:, :, None] * inverse
    cosine = jnp.cos(angle)
    sine = jnp.sin(angle) * jnp.asarray(np.where(np.arange(128) % 64 < 32, -1.0, 1.0), jnp.float32)
    came_second = first.step(cosine, sine)
    frames_parts = to_group(after(frames_pair, *came))
    first.step(frames_pair[1])
    x_all, mean_one, inv_one = prep(me, frames_parts)
    first.step(x_all)
    second.step(*came_second)
    ring_qkv, w_own, vectors = join(
        join_first_kernel,
        me,
        first.blocks,
        (
            jax.ShapeDtypeStruct((8, 768, 128), jnp.bfloat16),
            jax.ShapeDtypeStruct((8, OWN, 128), jnp.bfloat16),
            jax.ShapeDtypeStruct((6, D), jnp.float32),
        ),
        "join_first",
        [pltpu.VMEM((8, SLAB, 128), jnp.bfloat16)],
    )

    w_pair = to_pair(w_own)
    x_all, ring_qkv = after((x_all, ring_qkv), *second.next, cot_pair[1])
    came = second.step(ring_qkv)
    a_low, w_qkv, low, attn_own, lse = front(x_all, mean_one, inv_one, ring_qkv, vectors, order, cosine, sine, lengths)
    attn_pair = to_pair(attn_own, *came, w_pair[1])
    w_out = join_out(to_group(w_pair, attn_own))
    came = second.step(attn_own)
    attn_parts = to_group(attn_pair, w_out)
    attn_parts = attn_parts[:2] + after(attn_parts[2:], *came)
    c_low, branch_seq = mix(x_all, attn_parts, w_out, vectors)
    third.step(*attn_parts[2:])
    came = second.step(*attn_parts[2:])
    second.blocks[7:] = after(came, c_low)
    came = third.next
    blocks = [block.reshape(-1, 2, 64, 128) for block in second.blocks]
    shape = jax.ShapeDtypeStruct((4, 16, 64, 512), jnp.bfloat16)
    w_gate_up = join(functools.partial(join_gate_up_kernel, slice(0, 9)), me, blocks, shape, "join_gate_up", space=HBM)
    w_gate_up = w_gate_up.reshape(4, 1024, 512)
    cot_parts = to_group(cot_pair, c_low)
    gate_up, hidden = gate_step(after(c_low, *came), w_gate_up)
    came = third.step(c_low)
    g_down, d_mlp = down_grad(me, after(hidden, *came), cot_parts, vectors)
    third.step(hidden)
    third.step(g_down)
    shape = jax.ShapeDtypeStruct((1024, D), jnp.bfloat16)
    third.blocks[0] = after(third.blocks[0], g_down)
    w_down = join_twice(join_down_kernel, me, third.blocks, shape, "join_down")

    down = Scatter(g_down, device)
    d_both = hidden_back(gate_up, d_mlp, w_down)
    came = down.step(*third.next)
    d_both = after(d_both, *came)
    d_c_parts = norm_back(me, d_both, w_gate_up)
    came = down.step(d_both)
    d_c_sent, d_c_kept = half_sum(*after(tuple(d_c_parts), *came))
    g_gate_up = gate_grad(c_low, after(d_both, d_c_sent, d_c_kept))
    came = down.step(d_c_sent, hold=(g_gate_up,))
    gate_grads = Scatter(g_gate_up, device)

    x_own = frames[0].astype(jnp.float32)
    cot_own = cotangent[0].astype(jnp.float32)
    branch_own = jnp.where(y == 0, branch_seq[:256], branch_seq[256:])
    mid_own = x_own + vectors[4] * branch_own
    normed_two, scale_two = normed_of(mid_own)
    d_c_own = full_sum(d_c_sent, d_c_kept)
    d_mid = cot_own + norm_rows_back(d_c_own, normed_two, scale_two, vectors[2])
    d_branch_own = (d_mid * vectors[4]).astype(jnp.bfloat16)
    d_branch_pair = to_pair(d_branch_own)
    down.step(hold=(d_branch_own,))
    came = gate_grads.step(hold=(d_branch_own,))
    hidden = after(hidden, d_branch_own, *came)
    *out_parts, g_scale_mlp = out_step(me, hidden, w_down, cot_parts)
    came = gate_grads.step(d_branch_own, hold=(g_scale_mlp,))
    d_branch = to_group(d_branch_pair, *came, g_scale_mlp)
    out_sent, out_kept = half_sum(*out_parts)
    g_gain_two = jnp.sum(d_c_own * normed_two, axis=0)
    g_bias_two = jnp.sum(d_c_own, axis=0)
    g_scale_attn = jnp.sum(d_mid * branch_own, axis=0)
    small = jnp.concatenate([jnp.stack([g_gain_two, g_bias_two, g_scale_attn]), g_scale_mlp], axis=0)

    d_branch = after(d_branch, small)
    d_qkv, g_out = attention_back(me, d_branch, w_own, attn_own, low, lse, cosine, sine, lengths)
    came = gate_grads.step(*d_branch, hold=(d_qkv,))
    out_sent = after(out_sent, *d_branch)
    output = (mid_own + vectors[5] * full_sum(out_sent, out_kept)).astype(jnp.bfloat16)
    d_qkv = after(d_qkv, *came)
    g_first, *d_a_parts = grad_step(me, a_low, w_qkv, order, d_qkv, g_out, x_all, mean_one, inv_one, small)
    came = gate_grads.step(d_qkv, hold=(g_first,))
    first_grads = Scatter(after(g_first, *came), device)
    first_grads.step(output)
    d_a_sent, d_a_kept = half_sum(*d_a_parts)
    first_grads.step(d_a_sent)
    first_grads.step()
    normed_one, scale_one = normed_of(x_own)
    d_one = norm_rows_back(full_sum(d_a_sent, d_a_kept), normed_one, scale_one, vectors[0])
    frames_grad = (d_mid + d_one).astype(jnp.bfloat16)
    first_grads.step(frames_grad)
    g_first, g_gate_up, g_down = first_grads.total, gate_grads.total, down.total

    main = jnp.concatenate([g_first[:1024], g_gate_up, g_down]).reshape(32, 128, 128)
    slab = jnp.concatenate([main[1:, :8], main[1:, 64:72]], axis=1)
    slab = jnp.concatenate([slab, g_first[None, 1024:]])
    pieces = jnp.concatenate([main, slab], axis=1)
    pieces = lax.all_to_all(pieces, EVERY, split_axis=0, concat_axis=0, tiled=True)
    params_grad = collect(pieces, me, params.shape[0])
    new_params, new_first, new_second = adam_update(params, params_grad, first_moment, second_moment)
    return (output[None], frames_grad[None], params_grad, new_params, new_first, new_second)


def solution(mesh):
    def run(frames, cotangent, clip_lengths, params, first_moment, second_moment):
        fits = (
            mesh.shape["dp"] == 16
            and mesh.shape["seq"] == 2
            and frames.shape == (16, 512, D)
            and clip_lengths.shape == (16, 2)
        )
        if fits:
            over = Mesh(mesh.devices.reshape(4, 2, 2, 2), EVERY)
            rows, clips, flat = P(("z", "x", "c"), "y", None), P(("z", "x", "c"), None), P(EVERY)
        else:
            over = mesh
            rows, clips, flat = P("dp", "seq", None), P("dp", None), P(("dp", "seq"))
        step = jax.shard_map(
            fast_body if fits else body,
            mesh=over,
            in_specs=(rows, rows, clips, flat, flat, flat),
            out_specs=(rows, rows, flat, flat, flat, flat),
            check_vma=False,
        )
        return step(frames, cotangent, clip_lengths, params, first_moment, second_moment)

    return run
```

profile of v0, /device:TPU:1, one launch (start us, length us, event | category | flops | bytes accessed | tf_op | source)
XLA Modules:
  0.0 308.4 jit_solution(4555913959689900734)
XLA Ops:
  0.6 1.7 pad_bitcast_fusion.flat_ref
  2.4 3.6 %spread.1 = bf16[32,144,128]{2,1,0:T(8,128)(2,1)} custom-call(s32[1]{0:T(128)} %bitcast.1.me_ref.y_ref, f32[4224,128]{1,0:T(8,128)S(1)} %pad_bitcast_fusion.flat_ref), custom_call_target="tpu_custom_call" | custom-call | tf_op jit(solution)/shard_map/spread/pallas_call | solution.py:433
  6.0 7.2 %all-to-all-start = ((bf16[32,144,128]{2,1,0:T(8,128)(2,1)}), bf16[32,144,128]{2,1,0:T(8,128)(2,1)S(1)}, u32[]{:S(2)}, u32[]{:S(2)}) async-start(bf16[32,144,128]{2,1,0:T(8,128)(2,1)} %spread.1), calls=%async_computation | async-start | bytes 2359296 | tf_op jit(solution)/shard_map/all_to_all | solution.py:1254
  13.6 28.2 %all-to-all-done.piece_ref = bf16[32,144,128]{2,1,0:T(8,128)(2,1)S(1)} async-done(((bf16[32,144,128]{2,1,0:T(8,128)(2,1)}), bf16[32,144,128]{2,1,0:T(8,128)(2,1)S(1)}, u32[]{:S(2)}, u32[]{:S(2)}) %all-to-all-start) | async-done | bytes 1179680 | tf_op jit(solution)/shard_map/all_to_all | solution.py:1254
  41.9 1.8 collective-permute-start
  44.7 1.9 fusion.23
  46.6 3.3 %collective-permute-done.refs_1_ = bf16[1040,128]{1,0:T(8,128)(2,1)S(1)} collective-permute-done((bf16[1040,128]{1,0:T(8,128)(2,1)S(1)}, bf16[1040,128]{1,0:T(8,128)(2,1)S(1)}, u32[]{:S(2)}, u32[]{:S(2)}) %collective-permute-start) | collective-permute-done | bytes 266272 | tf_op jit(solution)/shard_map/ppermute | solution.py:1155
  49.9 2.0 collective-permute-done.1.refs_2_
  51.9 1.5 collective-permute-start.4
  53.4 6.5 %collective-permute-done.3.refs_3_ = bf16[1040,128]{1,0:T(8,128)(2,1)S(1)} collective-permute-done((bf16[1040,128]{1,0:T(8,128)(2,1)S(1)}, bf16[1040,128]{1,0:T(8,128)(2,1)S(1)}, u32[]{:S(2)}, u32[]{:S(2)}) %collective-permute-start.3) | collective-permute-done | bytes 266272 | tf_op jit(solution)/shard_map/ppermute | solution.py:1155
  59.9 1.5 collective-permute-start.7
  61.3 1.4 collective-permute-start.8
  62.8 4.2 %collective-permute-done.6.refs_5_ = bf16[1040,128]{1,0:T(8,128)(2,1)S(1)} collective-permute-done((bf16[1040,128]{1,0:T(8,128)(2,1)S(1)}, bf16[1040,128]{1,0:T(8,128)(2,1)S(1)}, u32[]{:S(2)}, u32[]{:S(2)}) %collective-permute-start.6) | collective-permute-done | bytes 266272 | tf_op jit(solution)/shard_map/ppermute | solution.py:1155
  70.5 7.7 %collective-permute-done.12 = bf16[2048,128]{1,0:T(8,128)(2,1)S(1)} collective-permute-done((bf16[2048,128]{1,0:T(8,128)(2,1)S(1)}, bf16[2048,128]{1,0:T(8,128)(2,1)S(1)}, u32[]{:S(2)}, u32[]{:S(2)}) %collective-permute-start.12) | collective-permute-done | bytes 524320 | tf_op jit(solution)/shard_map/ppermute | solution.py:1155
  78.3 1.9 collective-permute-done.11.refs_8_
  81.7 1.6 collective-permute-start.16
  83.4 10.6 %front.1 = (bf16[1024,1024]{1,0:T(8,128)(2,1)}, bf16[1024,768]{1,0:T(8,128)(2,1)}, bf16[1024,768]{1,0:T(8,128)(2,1)}, bf16[1024,256]{1,0:T(8,128)(2,1)S(1)}, f32[1024,4]{1,0:T(8,128)}) custom-call(bf16[1024,1024]{1,0:T(8,128)(2,1)S(1)} %get-tuple-element.217.x_ref, f32[1024,1]{1,0:T(8,128)S(1)} %get-tuple-element.218.mean_ref, ...), custom_call_target="tpu_custom_call" | custom-call | flops 12884901888 | bytes 8388608 | tf_op jit(solution)/shard_map/front/pallas_call | solution.py:806
  94.1 3.6 %collective-permute-start.19 = (bf16[8,256,128]{2,1,0:T(8,128)(2,1)S(1)}, bf16[8,256,128]{2,1,0:T(8,128)(2,1)S(1)}, u32[]{:S(2)}, u32[]{:S(2)}) collective-permute-start(bf16[8,256,128]{2,1,0:T(8,128)(2,1)S(1)} %get-tuple-element.228.refs_0_.ring_ref), channel_id=1, source_target_pairs={{0,2},{2,0},{1,3},{3,1},{4,6},{6,4},{5,7},{7,5},{8,10},{10,8},{9,1... | collective-permute-start | bytes 1572872 | tf_op jit(solution)/shard_map/ppermute | solution.py:1215
  97.7 1.7 collective-permute-start.18
  99.5 1.4 collective-permute-start.24
  101.5 9.8 %collective-permute-done.18.pair_ref = bf16[1024,256]{1,0:T(8,128)(2,1)S(1)} collective-permute-done((bf16[1024,256]{1,0:T(8,128)(2,1)S(1)}, bf16[1024,256]{1,0:T(8,128)(2,1)S(1)}, u32[]{:S(2)}, u32[]{:S(2)}) %collective-permute-start.18) | collective-permute-done | bytes 524320 | tf_op jit(solution)/shard_map/ppermute | solution.py:1210
  112.6 1.3 collective-permute-done.21.far_ref
  114.7 1.4 collective-permute-start.26
  117.6 1.8 collective-permute-start.28
  119.5 3.3 %mix.1 = (bf16[1024,1024]{1,0:T(8,128)(2,1)S(1)}, f32[512,1024]{1,0:T(8,128)S(1)}) custom-call(bf16[1024,1024]{1,0:T(8,128)(2,1)S(1)} %get-tuple-element.217.x_ref, bf16[1024,256]{1,0:T(8,128)(2,1)S(1)} %get-tuple-element.230.own_ref.attn_ref, bf16[1024,256]{1,0:T(8,128)(2,1)S(1)} %collective-permute-done.18.pair_ref, ...), custom_call_target="tpu_custom_call" | custom-call | flops 3221225472 | bytes 10485760 | tf_op jit(solution)/shard_map/mix/pallas_call | solution.py:844
  122.8 1.3 copy-done.24
  124.1 1.5 collective-permute-start.31
  126.4 1.5 collective-permute-done.27
  128.7 2.6 join_gate_up.1
  131.6 4.5 %gate.1 = (f32[4,1024,512]{2,1,0:T(8,128)S(1)}, bf16[1024,1024]{1,0:T(8,128)(2,1)S(1)}) custom-call(bf16[1024,1024]{1,0:T(8,128)(2,1)S(1)} %copy-done.25, bf16[4,1024,512]{2,1,0:T(8,128)(2,1)S(1)} %bitcast.127), custom_call_target="tpu_custom_call" | custom-call | flops 5368709120 | bytes 16777216 | tf_op jit(solution)/shard_map/gate/pallas_call | solution.py:871
  137.6 3.9 %down_grad.1 = (bf16[8,1024,128]{2,1,0:T(8,128)(2,1)S(1)}, bf16[1024,1024]{1,0:T(8,128)(2,1)S(1)}) custom-call(s32[1]{0:T(128)} %bitcast.1.me_ref.y_ref, bf16[1024,1024]{1,0:T(8,128)(2,1)S(1)} %get-tuple-element.298.hidden_ref, bf16[256,1024]{1,0:T(8,128)(2,1)S(1)} %bitcast.131, bf16[256,1024]{1,0:T(8,128)(2,1)} %collective-permute-done.14.pair_ref, ...), custom_call_target="tpu_custom_call" | custom-call | flops 3221225472 | bytes 8388608 | tf_op jit(solution)/shard_map/down_grad/pallas_call | solution.py:900
  143.2 1.2 collective-permute-start.36
  144.6 1.7 join_down.1._
  147.3 1.5 collective-permute-start.38
  149.1 3.8 %hidden_back.1.d_both_ref = bf16[4,1024,512]{2,1,0:T(8,128)(2,1)S(1)} custom-call(f32[4,1024,512]{2,1,0:T(8,128)S(1)} %get-tuple-element.253.gate_up_ref, bf16[1024,1024]{1,0:T(8,128)(2,1)S(1)} %get-tuple-element.261.d_mlp_ref, bf16[1024,1024]{1,0:T(8,128)(2,1)S(1)} %join_down_rest.1.w_ref), custom_call_target="tpu_custom_call" | custom-call | flops 4294967296 | bytes 18874368 | tf_op jit(solution)/shard_map/hidden_back/pallas_call | solution.py:943
  153.2 1.3 collective-permute-start.40
  154.5 4.9 %norm_back.1 = (f32[256,1024]{1,0:T(8,128)S(1)}, f32[256,1024]{1,0:T(8,128)S(1)}, bf16[256,1024]{1,0:T(8,128)(2,1)S(1)}, bf16[256,1024]{1,0:T(8,128)(2,1)S(1)}) custom-call(s32[1]{0:T(128)} %bitcast.1.me_ref.y_ref, bf16[4,1024,512]{2,1,0:T(8,128)(2,1)S(1)} %hidden_back.1.d_both_ref, bf16[4,1024,512]{2,1,0:T(8,128)(2,1)S(1)} %bitcast.128), custom_call_target="tpu_custom_call" | custom-call | flops 5368709120 | bytes 12582912 | tf_op jit(solution)/shard_map/norm_back/pallas_call | solution.py:965
  159.5 5.5 %collective-permute-start.42 = (bf16[256,1024]{1,0:T(8,128)(2,1)S(1)}, bf16[256,1024]{1,0:T(8,128)(2,1)S(1)}, u32[]{:S(2)}, u32[]{:S(2)}) collective-permute-start(bf16[256,1024]{1,0:T(8,128)(2,1)S(1)} %get-tuple-element.290), channel_id=1, source_target_pairs={{0,2},{2,0},{1,3},{3,1},{4,6},{6,4},{5,7},{7,5},{8,10},{10,8},{9,1... | collective-permute-start | bytes 1572872 | tf_op jit(solution)/shard_map/ppermute | solution.py:1220
  167.6 1.5 collective-permute-start.43
  169.1 4.5 %gate_grad.1 = bf16[8,2048,128]{2,1,0:T(8,128)(2,1)S(1)} custom-call(bf16[1024,1024]{1,0:T(8,128)(2,1)S(1)} %copy-done.25, bf16[4,1024,512]{2,1,0:T(8,128)(2,1)S(1)} %hidden_back.1.d_both_ref), custom_call_target="tpu_custom_call" | custom-call | flops 5368709120 | bytes 10485760 | tf_op jit(solution)/shard_map/gate_grad/pallas_call | solution.py:991
  173.8 1.5 collective-permute-start.44
  178.3 3.4 %collective-permute-done.44 = bf16[1024,128]{1,0:T(8,128)(2,1)S(1)} collective-permute-done((bf16[1024,128]{1,0:T(8,128)(2,1)S(1)}, bf16[1024,128]{1,0:T(8,128)(2,1)S(1)}, u32[]{:S(2)}, u32[]{:S(2)}) %collective-permute-start.44) | collective-permute-done | bytes 262176 | tf_op jit(solution)/shard_map/ppermute | solution.py:1155
  187.2 6.3 %out.1 = (f32[256,1024]{1,0:T(8,128)}, f32[256,1024]{1,0:T(8,128)}, bf16[256,1024]{1,0:T(8,128)(2,1)S(1)}, bf16[256,1024]{1,0:T(8,128)(2,1)}, f32[1,1024]{1,0:T(1,128)S(1)}) custom-call(s32[1]{0:T(128)} %bitcast.1.me_ref.y_ref, bf16[1024,1024]{1,0:T(8,128)(2,1)S(1)} %get-tuple-element.298.hidden_ref, bf16[1024,1024]{1,0:T(8,128)(2,1)S(1)} %join_down_rest.1.w_ref, ...), custom_call_target="tpu_custom_call" | custom-call | flops 3221225472 | bytes 10485760 | tf_op jit(solution)/shard_map/out/pallas_call | solution.py:1019
  193.5 3.7 %collective-permute-start.47 = (bf16[256,1024]{1,0:T(8,128)(2,1)}, bf16[256,1024]{1,0:T(8,128)(2,1)S(1)}, u32[]{:S(2)}, u32[]{:S(2)}) collective-permute-start(bf16[256,1024]{1,0:T(8,128)(2,1)} %get-tuple-element.302), channel_id=1, source_target_pairs={{0,2},{2,0},{1,3},{3,1},{4,6},{6,4},{5,7},{7,5},{8,10},{10,8},{9,1... | collective-permute-start | bytes 1572872 | tf_op jit(solution)/shard_map/ppermute | solution.py:1220
  197.4 1.4 fusion.24
  200.4 2.1 collective-permute-start.51
  202.5 1.5 convert_add_fusion.7
  205.0 1.6 fusion.15
  209.6 11.7 %attend_back.1 = (bf16[1024,768]{1,0:T(8,128)(2,1)S(1)}, bf16[8,256,128]{2,1,0:T(8,128)(2,1)S(1)}) custom-call(s32[1]{0:T(128)} %bitcast.1.me_ref.y_ref, bf16[256,1024]{1,0:T(8,128)(2,1)S(1)} %multiply_convert_fusion.own_ref, bf16[256,1024]{1,0:T(8,128)(2,1)S(1)} %collective-permute-done.48.pair_ref, bf16[256,1024]{1,0:T(8,128)(2,1)S(1)} %collective-permute-done.51.far_ref, ...), custom_call_target="tpu_custom_call" | custom-call | flops 12884901888 | bytes 10485760 | tf_op jit(solution)/shard_map/attend_back/pallas_call | solution.py:1084
  221.6 1.1 collective-permute-start.59
  223.3 6.9 %grad.1 = (bf16[8,1040,128]{2,1,0:T(8,128)(2,1)S(1)}, f32[256,1024]{1,0:T(8,128)S(1)}, f32[256,1024]{1,0:T(8,128)S(1)}, bf16[256,1024]{1,0:T(8,128)(2,1)S(1)}, bf16[256,1024]{1,0:T(8,128)(2,1)S(1)}) custom-call(s32[1]{0:T(128)} %bitcast.1.me_ref.y_ref, bf16[1024,1024]{1,0:T(8,128)(2,1)S(1)} %copy-done.26, bf16[1024,768]{1,0:T(8,128)(2,1)S(1)} %copy-done.27, ...), custom_call_target="tpu_custom_call" | custom-call | flops 8589934592 | bytes 12582912 | tf_op jit(solution)/shard_map/grad/pallas_call | solution.py:1136
  230.2 1.9 collective-permute-start.57
  233.8 2.2 collective-permute-start.56
  237.9 3.3 %collective-permute-done.62 = bf16[512,128]{1,0:T(8,128)(2,1)S(1)} collective-permute-done((bf16[512,128]{1,0:T(8,128)(2,1)S(1)}, bf16[512,128]{1,0:T(8,128)(2,1)S(1)}, u32[]{:S(2)}, u32[]{:S(2)}) %collective-permute-start.62) | collective-permute-done | bytes 131104 | tf_op jit(solution)/shard_map/ppermute | solution.py:1155
  244.5 2.7 collective-permute-done.63
  248.0 1.5 collective-permute-start.65
  249.5 4.2 %collective-permute-done.58 = bf16[256,1024]{1,0:T(8,128)(2,1)S(1)} collective-permute-done((bf16[256,1024]{1,0:T(8,128)(2,1)S(1)}, bf16[256,1024]{1,0:T(8,128)(2,1)S(1)}, u32[]{:S(2)}, u32[]{:S(2)}) %collective-permute-start.58) | collective-permute-done | bytes 524320 | tf_op jit(solution)/shard_map/ppermute | solution.py:1225
  254.2 1.3 fusion.9
  255.6 1.5 collective-permute-start.67
  257.4 3.6 %collective-permute-done.67 = bf16[1040,128]{1,0:T(8,128)(2,1)S(1)} collective-permute-done((bf16[1040,128]{1,0:T(8,128)(2,1)S(1)}, bf16[1040,128]{1,0:T(8,128)(2,1)S(1)}, u32[]{:S(2)}, u32[]{:S(2)}) %collective-permute-start.67) | collective-permute-done | bytes 266272 | tf_op jit(solution)/shard_map/ppermute | solution.py:1155
  260.9 1.4 collective-permute-done.68
  262.8 38.5 %all_to_all.10.piece_ref = bf16[32,144,128]{2,1,0:T(8,128)(2,1)S(1)} all-to-all(bf16[32,144,128]{2,1,0:T(8,128)(2,1)S(1)} %maximum_maximum_fusion), channel_id=1, replica_groups=mesh['z'=4,'x'=2,'c'=2,'y'=2] {'z','x','c','y'}, dimensions={0} | all-to-all | bytes 2359296 | tf_op jit(solution)/shard_map/all_to_all | solution.py:1373
  301.3 2.9 collect.1
  304.2 4.0 %multiply_subtract_fusion = (f32[524480]{0:T(1024)}, f32[524480]{0:T(1024)}, f32[524480]{0:T(1024)}, f32[524480]{0:T(1024)}) fusion(f32[524480]{0:T(1024)S(1)} %copy-done.34, f32[524480]{0:T(1024)S(1)} %copy-done.35, f32[524480]{0:T(1024)S(1)} %copy-done.36, f32[525312]{0:T(1024)S(1)} %bitcast.126), kind=kLoop, calls=%fused_computation.3 | loop fusion | flops 7867200 | bytes 16783360 | tf_op jit(solution)/shard_map/sub | solution.py:141
  (270 shorter events, 43.8 us)
Async XLA Ops:
  6.0 35.8 %all-to-all-start = ((bf16[32,144,128]{2,1,0:T(8,128)(2,1)}), bf16[32,144,128]{2,1,0:T(8,128)(2,1)S(1)}, u32[]{:S(2)}, u32[]{:S(2)}) async-start(bf16[32,144,128]{2,1,0:T(8,128)(2,1)} %spread.1), calls=%async_computation | async-start | bytes 2359296 | tf_op jit(solution)/shard_map/all_to_all | solution.py:1254
  13.3 30.6 %collective-permute-start.2 = (s32[1,2]{1,0:T(1,128)S(1)}, s32[1,2]{1,0:T(1,128)S(1)}, u32[]{:S(2)}, u32[]{:S(2)}) collective-permute-start(s32[1,2]{1,0:T(1,128)S(1)} %copy-done.13), channel_id=1, source_target_pairs={{0,2},{2,0},{1,3},{3,1},{4,6},{6,4},{5,7},{7,5},{8,10},{10,8},{9,1... | collective-permute-start | bytes 32 | tf_op jit(solution)/shard_map/ppermute | solution.py:1247
  41.9 8.0 %collective-permute-start = (bf16[1040,128]{1,0:T(8,128)(2,1)S(1)}, bf16[1040,128]{1,0:T(8,128)(2,1)S(1)}, u32[]{:S(2)}, u32[]{:S(2)}) collective-permute-start(bf16[1040,128]{1,0:T(8,128)(2,1)S(1)} %get-tuple-element.188.refs_0_), channel_id=1, source_target_pairs={{0,8},{8,16},{16,24},{24,28},{28,20},{20,12},{12,4},{4,0},{1,9},{9... | collective-permute-start | bytes 798728 | tf_op jit(solution)/shard_map/ppermute | solution.py:1155
  43.8 8.1 %collective-permute-start.1 = (bf16[1040,128]{1,0:T(8,128)(2,1)S(1)}, bf16[1040,128]{1,0:T(8,128)(2,1)S(1)}, u32[]{:S(2)}, u32[]{:S(2)}) collective-permute-start(bf16[1040,128]{1,0:T(8,128)(2,1)S(1)} %get-tuple-element.188.refs_0_), channel_id=1, source_target_pairs={{8,0},{16,8},{24,16},{28,24},{20,28},{12,20},{4,12},{0,4},{9,1},{1... | collective-permute-start | bytes 798728 | tf_op jit(solution)/shard_map/ppermute | solution.py:1155
  44.1 15.8 %collective-permute-start.5 = (bf16[256,1024]{1,0:T(8,128)(2,1)S(1)}, bf16[256,1024]{1,0:T(8,128)(2,1)S(1)}, u32[]{:S(2)}, u32[]{:S(2)}) collective-permute-start(bf16[256,1024]{1,0:T(8,128)(2,1)S(1)} %bitcast.123), channel_id=1, source_target_pairs={{0,1},{1,0},{2,3},{3,2},{4,5},{5,4},{6,7},{7,6},{8,9},{9,8},{10,11... | collective-permute-start | bytes 1572872 | tf_op jit(solution)/shard_map/ppermute | solution.py:1210
  51.9 8.0 %collective-permute-start.3 = (bf16[1040,128]{1,0:T(8,128)(2,1)S(1)}, bf16[1040,128]{1,0:T(8,128)(2,1)S(1)}, u32[]{:S(2)}, u32[]{:S(2)}) collective-permute-start(bf16[1040,128]{1,0:T(8,128)(2,1)S(1)} %collective-permute-done.refs_1_), channel_id=1, source_target_pairs={{0,8},{8,16},{16,24},{24,28},{28,20},{20,12},{12,4},{4,0},{1,9},{9... | collective-permute-start | bytes 798728 | tf_op jit(solution)/shard_map/ppermute | solution.py:1155
  51.9 8.0 %collective-permute-start.4 = (bf16[1040,128]{1,0:T(8,128)(2,1)S(1)}, bf16[1040,128]{1,0:T(8,128)(2,1)S(1)}, u32[]{:S(2)}, u32[]{:S(2)}) collective-permute-start(bf16[1040,128]{1,0:T(8,128)(2,1)S(1)} %collective-permute-done.1.refs_2_), channel_id=1, source_target_pairs={{8,0},{16,8},{24,16},{28,24},{20,28},{12,20},{4,12},{0,4},{9,1},{1... | collective-permute-start | bytes 798728 | tf_op jit(solution)/shard_map/ppermute | solution.py:1155
  59.9 7.0 %collective-permute-start.6 = (bf16[1040,128]{1,0:T(8,128)(2,1)S(1)}, bf16[1040,128]{1,0:T(8,128)(2,1)S(1)}, u32[]{:S(2)}, u32[]{:S(2)}) collective-permute-start(bf16[1040,128]{1,0:T(8,128)(2,1)S(1)} %collective-permute-done.3.refs_3_), channel_id=1, source_target_pairs={{0,8},{8,16},{16,24},{24,28},{28,20},{20,12},{12,4},{4,0},{1,9},{9... | collective-permute-start | bytes 798728 | tf_op jit(solution)/shard_map/ppermute | solution.py:1155
  59.9 7.8 %collective-permute-start.7 = (bf16[1040,128]{1,0:T(8,128)(2,1)S(1)}, bf16[1040,128]{1,0:T(8,128)(2,1)S(1)}, u32[]{:S(2)}, u32[]{:S(2)}) collective-permute-start(bf16[1040,128]{1,0:T(8,128)(2,1)S(1)} %collective-permute-done.4.refs_4_), channel_id=1, source_target_pairs={{8,0},{16,8},{24,16},{28,24},{20,28},{12,20},{4,12},{0,4},{9,1},{1... | collective-permute-start | bytes 798728 | tf_op jit(solution)/shard_map/ppermute | solution.py:1155
  61.3 6.5 %collective-permute-start.8 = (bf16[256,1024]{1,0:T(8,128)(2,1)S(1)}, bf16[256,1024]{1,0:T(8,128)(2,1)S(1)}, u32[]{:S(2)}, u32[]{:S(2)}) collective-permute-start(bf16[256,1024]{1,0:T(8,128)(2,1)S(1)} %bitcast.124), channel_id=1, source_target_pairs={{0,2},{2,0},{1,3},{3,1},{4,6},{6,4},{5,7},{7,5},{8,10},{10,8},{9,1... | collective-permute-start | bytes 1572872 | tf_op jit(solution)/shard_map/ppermute | solution.py:1215
  62.7 15.5 %collective-permute-start.12 = (bf16[2048,128]{1,0:T(8,128)(2,1)S(1)}, bf16[2048,128]{1,0:T(8,128)(2,1)S(1)}, u32[]{:S(2)}, u32[]{:S(2)}) collective-permute-start(bf16[2048,128]{1,0:T(8,128)(2,1)S(1)} %get-tuple-element.213), channel_id=1, source_target_pairs={{0,8},{8,16},{16,24},{24,28},{28,20},{20,12},{12,4},{4,0},{1,9},{9... | collective-permute-start | bytes 1572872 | tf_op jit(solution)/shard_map/ppermute | solution.py:1155
  66.9 11.3 %collective-permute-start.13 = (bf16[2048,128]{1,0:T(8,128)(2,1)S(1)}, bf16[2048,128]{1,0:T(8,128)(2,1)S(1)}, u32[]{:S(2)}, u32[]{:S(2)}) collective-permute-start(bf16[2048,128]{1,0:T(8,128)(2,1)S(1)} %get-tuple-element.213), channel_id=1, source_target_pairs={{8,0},{16,8},{24,16},{28,24},{20,28},{12,20},{4,12},{0,4},{9,1},{1... | collective-permute-start | bytes 1572872 | tf_op jit(solution)/shard_map/ppermute | solution.py:1155
  67.7 13.9 %collective-permute-start.14 = (bf16[256,1024]{1,0:T(8,128)(2,1)S(1)}, bf16[256,1024]{1,0:T(8,128)(2,1)}, u32[]{:S(2)}, u32[]{:S(2)}) collective-permute-start(bf16[256,1024]{1,0:T(8,128)(2,1)S(1)} %bitcast.129), channel_id=1, source_target_pairs={{0,1},{1,0},{2,3},{3,2},{4,5},{5,4},{6,7},{7,6},{8,9},{9,8},{10,11... | collective-permute-start | bytes 1572872 | tf_op jit(solution)/shard_map/ppermute | solution.py:1210
  69.0 12.2 %collective-permute-start.10 = (bf16[528,128]{1,0:T(8,128)(2,1)S(1)}, bf16[528,128]{1,0:T(8,128)(2,1)S(1)}, u32[]{:S(2)}, u32[]{:S(2)}) collective-permute-start(bf16[528,128]{1,0:T(8,128)(2,1)S(1)} %slice.64), channel_id=1, source_target_pairs={{0,8},{8,16},{16,24},{24,28},{28,20},{20,12},{12,4},{4,0},{1,9},{9... | collective-permute-start | bytes 405512 | tf_op jit(solution)/shard_map/ppermute | solution.py:1155
  69.7 10.4 %collective-permute-start.11 = (bf16[512,128]{1,0:T(8,128)(2,1)S(1)}, bf16[512,128]{1,0:T(8,128)(2,1)S(1)}, u32[]{:S(2)}, u32[]{:S(2)}) collective-permute-start(bf16[512,128]{1,0:T(8,128)(2,1)S(1)} %slice.65), channel_id=1, source_target_pairs={{8,0},{16,8},{24,16},{28,24},{20,28},{12,20},{4,12},{0,4},{9,1},{1... | collective-permute-start | bytes 393224 | tf_op jit(solution)/shard_map/ppermute | solution.py:1155
  81.7 12.4 %collective-permute-start.15 = (bf16[2048,128]{1,0:T(8,128)(2,1)S(1)}, bf16[2048,128]{1,0:T(8,128)(2,1)S(1)}, u32[]{:S(2)}, u32[]{:S(2)}) collective-permute-start(bf16[2048,128]{1,0:T(8,128)(2,1)S(1)} %collective-permute-done.12), channel_id=1, source_target_pairs={{0,8},{8,16},{16,24},{24,28},{28,20},{20,12},{12,4},{4,0},{1,9},{9... | collective-permute-start | bytes 1572872 | tf_op jit(solution)/shard_map/ppermute | solution.py:1155
  81.7 12.4 %collective-permute-start.16 = (bf16[2048,128]{1,0:T(8,128)(2,1)S(1)}, bf16[2048,128]{1,0:T(8,128)(2,1)S(1)}, u32[]{:S(2)}, u32[]{:S(2)}) collective-permute-start(bf16[2048,128]{1,0:T(8,128)(2,1)S(1)} %collective-permute-done.13), channel_id=1, source_target_pairs={{8,0},{16,8},{24,16},{28,24},{20,28},{12,20},{4,12},{0,4},{9,1},{1... | collective-permute-start | bytes 1572872 | tf_op jit(solution)/shard_map/ppermute | solution.py:1155
  83.4 10.8 %collective-permute-start.17 = (bf16[8,256,128]{2,1,0:T(8,128)(2,1)S(1)}, bf16[8,256,128]{2,1,0:T(8,128)(2,1)S(1)}, u32[]{:S(2)}, u32[]{:S(2)}) collective-permute-start(bf16[8,256,128]{2,1,0:T(8,128)(2,1)S(1)} %get-tuple-element.228.refs_0_.ring_ref), channel_id=1, source_target_pairs={{0,1},{1,0},{2,3},{3,2},{4,5},{5,4},{6,7},{7,6},{8,9},{9,8},{10,11... | collective-permute-start | bytes 1572872 | tf_op jit(solution)/shard_map/ppermute | solution.py:1210
  94.1 6.8 %collective-permute-start.19 = (bf16[8,256,128]{2,1,0:T(8,128)(2,1)S(1)}, bf16[8,256,128]{2,1,0:T(8,128)(2,1)S(1)}, u32[]{:S(2)}, u32[]{:S(2)}) collective-permute-start(bf16[8,256,128]{2,1,0:T(8,128)(2,1)S(1)} %get-tuple-element.228.refs_0_.ring_ref), channel_id=1, source_target_pairs={{0,2},{2,0},{1,3},{3,1},{4,6},{6,4},{5,7},{7,5},{8,10},{10,8},{9,1... | collective-permute-start | bytes 1572872 | tf_op jit(solution)/shard_map/ppermute | solution.py:1215
  97.7 13.6 %collective-permute-start.18 = (bf16[1024,256]{1,0:T(8,128)(2,1)S(1)}, bf16[1024,256]{1,0:T(8,128)(2,1)S(1)}, u32[]{:S(2)}, u32[]{:S(2)}) collective-permute-start(bf16[1024,256]{1,0:T(8,128)(2,1)S(1)} %get-tuple-element.230.own_ref.attn_ref), channel_id=1, source_target_pairs={{0,1},{1,0},{2,3},{3,2},{4,5},{5,4},{6,7},{7,6},{8,9},{9,8},{10,11... | collective-permute-start | bytes 1572872 | tf_op jit(solution)/shard_map/ppermute | solution.py:1210
  99.5 13.0 %collective-permute-start.23 = (bf16[2048,128]{1,0:T(8,128)(2,1)S(1)}, bf16[2048,128]{1,0:T(8,128)(2,1)S(1)}, u32[]{:S(2)}, u32[]{:S(2)}) collective-permute-start(bf16[2048,128]{1,0:T(8,128)(2,1)S(1)} %collective-permute-done.15), channel_id=1, source_target_pairs={{0,8},{8,16},{16,24},{24,28},{28,20},{20,12},{12,4},{4,0},{1,9},{9... | collective-permute-start | bytes 1572872 | tf_op jit(solution)/shard_map/ppermute | solution.py:1155
  99.5 13.0 %collective-permute-start.24 = (bf16[2048,128]{1,0:T(8,128)(2,1)S(1)}, bf16[2048,128]{1,0:T(8,128)(2,1)S(1)}, u32[]{:S(2)}, u32[]{:S(2)}) collective-permute-start(bf16[2048,128]{1,0:T(8,128)(2,1)S(1)} %collective-permute-done.16), channel_id=1, source_target_pairs={{8,0},{16,8},{24,16},{28,24},{20,28},{12,20},{4,12},{0,4},{9,1},{1... | collective-permute-start | bytes 1572872 | tf_op jit(solution)/shard_map/ppermute | solution.py:1155
  114.6 10.9 %collective-permute-start.25 = (bf16[1024,128]{1,0:T(8,128)(2,1)S(1)}, bf16[1024,128]{1,0:T(8,128)(2,1)S(1)}, u32[]{:S(2)}, u32[]{:S(2)}) collective-permute-start(bf16[1024,128]{1,0:T(8,128)(2,1)S(1)} %get-tuple-element.271.refs_0_), channel_id=1, source_target_pairs={{0,8},{8,16},{16,24},{24,28},{28,20},{20,12},{12,4},{4,0},{1,9},{9... | collective-permute-start | bytes 786440 | tf_op jit(solution)/shard_map/ppermute | solution.py:1155
  114.7 11.6 %collective-permute-start.26 = (bf16[1024,128]{1,0:T(8,128)(2,1)S(1)}, bf16[1024,128]{1,0:T(8,128)(2,1)}, u32[]{:S(2)}, u32[]{:S(2)}) collective-permute-start(bf16[1024,128]{1,0:T(8,128)(2,1)S(1)} %get-tuple-element.271.refs_0_), channel_id=1, source_target_pairs={{8,0},{16,8},{24,16},{28,24},{20,28},{12,20},{4,12},{0,4},{9,1},{1... | collective-permute-start | bytes 786440 | tf_op jit(solution)/shard_map/ppermute | solution.py:1155
  116.8 11.1 %collective-permute-start.27 = (bf16[1024,128]{1,0:T(8,128)(2,1)}, bf16[1024,128]{1,0:T(8,128)(2,1)}, u32[]{:S(2)}, u32[]{:S(2)}) collective-permute-start(bf16[1024,128]{1,0:T(8,128)(2,1)} %slice.70), channel_id=1, source_target_pairs={{0,8},{8,16},{16,24},{24,28},{28,20},{20,12},{12,4},{4,0},{1,9},{9... | collective-permute-start | bytes 786440 | tf_op jit(solution)/shard_map/ppermute | solution.py:1155
  117.6 11.1 %collective-permute-start.28 = (bf16[1024,128]{1,0:T(8,128)(2,1)}, bf16[1024,128]{1,0:T(8,128)(2,1)}, u32[]{:S(2)}, u32[]{:S(2)}) collective-permute-start(bf16[1024,128]{1,0:T(8,128)(2,1)} %slice.71), channel_id=1, source_target_pairs={{8,0},{16,8},{24,16},{28,24},{20,28},{12,20},{4,12},{0,4},{9,1},{1... | collective-permute-start | bytes 786440 | tf_op jit(solution)/shard_map/ppermute | solution.py:1155
  124.1 13.6 %collective-permute-start.31 = (bf16[256,1024]{1,0:T(8,128)(2,1)S(1)}, bf16[256,1024]{1,0:T(8,128)(2,1)}, u32[]{:S(2)}, u32[]{:S(2)}) collective-permute-start(bf16[256,1024]{1,0:T(8,128)(2,1)S(1)} %bitcast.130), channel_id=1, source_target_pairs={{0,2},{2,0},{1,3},{3,1},{4,6},{6,4},{5,7},{7,5},{8,10},{10,8},{9,1... | collective-permute-start | bytes 1572872 | tf_op jit(solution)/shard_map/ppermute | solution.py:1215
  126.3 11.4 %collective-permute-start.32 = (bf16[256,1024]{1,0:T(8,128)(2,1)}, bf16[256,1024]{1,0:T(8,128)(2,1)}, u32[]{:S(2)}, u32[]{:S(2)}) collective-permute-start(bf16[256,1024]{1,0:T(8,128)(2,1)} %collective-permute-done.14.pair_ref), channel_id=1, source_target_pairs={{0,2},{2,0},{1,3},{3,1},{4,6},{6,4},{5,7},{7,5},{8,10},{10,8},{9,1... | collective-permute-start | bytes 1572872 | tf_op jit(solution)/shard_map/ppermute | solution.py:1215
  126.3 9.8 %collective-permute-start.29 = (bf16[1024,128]{1,0:T(8,128)(2,1)}, bf16[1024,128]{1,0:T(8,128)(2,1)S(1)}, u32[]{:S(2)}, u32[]{:S(2)}) collective-permute-start(bf16[1024,128]{1,0:T(8,128)(2,1)} %copy-done.46), channel_id=1, source_target_pairs={{0,8},{8,16},{16,24},{24,28},{28,20},{20,12},{12,4},{4,0},{1,9},{9... | collective-permute-start | bytes 786440 | tf_op jit(solution)/shard_map/ppermute | solution.py:1155
  127.9 8.2 %collective-permute-start.30 = (bf16[1024,128]{1,0:T(8,128)(2,1)}, bf16[1024,128]{1,0:T(8,128)(2,1)S(1)}, u32[]{:S(2)}, u32[]{:S(2)}) collective-permute-start(bf16[1024,128]{1,0:T(8,128)(2,1)} %collective-permute-done.26.refs_2_), channel_id=1, source_target_pairs={{8,0},{16,8},{24,16},{28,24},{20,28},{12,20},{4,12},{0,4},{9,1},{1... | collective-permute-start | bytes 786440 | tf_op jit(solution)/shard_map/ppermute | solution.py:1155
  136.1 6.4 %collective-permute-start.33 = (bf16[1024,128]{1,0:T(8,128)(2,1)S(1)}, bf16[1024,128]{1,0:T(8,128)(2,1)S(1)}, u32[]{:S(2)}, u32[]{:S(2)}) collective-permute-start(bf16[1024,128]{1,0:T(8,128)(2,1)S(1)} %collective-permute-done.29.refs_3_), channel_id=1, source_target_pairs={{0,8},{8,16},{16,24},{24,28},{28,20},{20,12},{12,4},{4,0},{1,9},{9... | collective-permute-start | bytes 786440 | tf_op jit(solution)/shard_map/ppermute | solution.py:1155
  136.8 6.0 %collective-permute-start.34 = (bf16[1024,128]{1,0:T(8,128)(2,1)S(1)}, bf16[1024,128]{1,0:T(8,128)(2,1)S(1)}, u32[]{:S(2)}, u32[]{:S(2)}) collective-permute-start(bf16[1024,128]{1,0:T(8,128)(2,1)S(1)} %collective-permute-done.30.refs_4_), channel_id=1, source_target_pairs={{8,0},{16,8},{24,16},{28,24},{20,28},{12,20},{4,12},{0,4},{9,1},{1... | collective-permute-start | bytes 786440 | tf_op jit(solution)/shard_map/ppermute | solution.py:1155
  147.1 5.8 %collective-permute-start.37 = (bf16[512,128]{1,0:T(8,128)(2,1)S(1)}, bf16[512,128]{1,0:T(8,128)(2,1)S(1)}, u32[]{:S(2)}, u32[]{:S(2)}) collective-permute-start(bf16[512,128]{1,0:T(8,128)(2,1)S(1)} %get-tuple-element.274), channel_id=1, source_target_pairs={{0,8},{8,16},{16,24},{24,28},{28,20},{20,12},{12,4},{4,0},{1,9},{9... | collective-permute-start | bytes 393224 | tf_op jit(solution)/shard_map/ppermute | solution.py:1155
  147.3 5.6 %collective-permute-start.38 = (bf16[512,128]{1,0:T(8,128)(2,1)S(1)}, bf16[512,128]{1,0:T(8,128)(2,1)S(1)}, u32[]{:S(2)}, u32[]{:S(2)}) collective-permute-start(bf16[512,128]{1,0:T(8,128)(2,1)S(1)} %get-tuple-element.275), channel_id=1, source_target_pairs={{8,0},{16,8},{24,16},{28,24},{20,28},{12,20},{4,12},{0,4},{9,1},{1... | collective-permute-start | bytes 393224 | tf_op jit(solution)/shard_map/ppermute | solution.py:1155
  153.0 6.4 %collective-permute-start.39 = (bf16[1024,128]{1,0:T(8,128)(2,1)S(1)}, bf16[1024,128]{1,0:T(8,128)(2,1)S(1)}, u32[]{:S(2)}, u32[]{:S(2)}) collective-permute-start(bf16[1024,128]{1,0:T(8,128)(2,1)S(1)} %get-tuple-element.283), channel_id=1, source_target_pairs={{0,8},{8,16},{16,24},{24,28},{28,20},{20,12},{12,4},{4,0},{1,9},{9... | collective-permute-start | bytes 786440 | tf_op jit(solution)/shard_map/ppermute | solution.py:1155
  153.2 6.2 %collective-permute-start.40 = (bf16[1024,128]{1,0:T(8,128)(2,1)S(1)}, bf16[1024,128]{1,0:T(8,128)(2,1)S(1)}, u32[]{:S(2)}, u32[]{:S(2)}) collective-permute-start(bf16[1024,128]{1,0:T(8,128)(2,1)S(1)} %get-tuple-element.284), channel_id=1, source_target_pairs={{8,0},{16,8},{24,16},{28,24},{20,28},{12,20},{4,12},{0,4},{9,1},{1... | collective-permute-start | bytes 786440 | tf_op jit(solution)/shard_map/ppermute | solution.py:1155
  159.5 7.1 %collective-permute-start.42 = (bf16[256,1024]{1,0:T(8,128)(2,1)S(1)}, bf16[256,1024]{1,0:T(8,128)(2,1)S(1)}, u32[]{:S(2)}, u32[]{:S(2)}) collective-permute-start(bf16[256,1024]{1,0:T(8,128)(2,1)S(1)} %get-tuple-element.290), channel_id=1, source_target_pairs={{0,2},{2,0},{1,3},{3,1},{4,6},{6,4},{5,7},{7,5},{8,10},{10,8},{9,1... | collective-permute-start | bytes 1572872 | tf_op jit(solution)/shard_map/ppermute | solution.py:1220
  167.6 14.7 %collective-permute-start.43 = (bf16[256,1024]{1,0:T(8,128)(2,1)S(1)}, bf16[256,1024]{1,0:T(8,128)(2,1)S(1)}, u32[]{:S(2)}, u32[]{:S(2)}) collective-permute-start(bf16[256,1024]{1,0:T(8,128)(2,1)S(1)} %add_convert_fusion.3), channel_id=1, source_target_pairs={{0,1},{1,0},{2,3},{3,2},{4,5},{5,4},{6,7},{7,6},{8,9},{9,8},{10,11... | collective-permute-start | bytes 1572872 | tf_op jit(solution)/shard_map/ppermute | solution.py:1225
  173.8 8.0 %collective-permute-start.44 = (bf16[1024,128]{1,0:T(8,128)(2,1)S(1)}, bf16[1024,128]{1,0:T(8,128)(2,1)S(1)}, u32[]{:S(2)}, u32[]{:S(2)}) collective-permute-start(bf16[1024,128]{1,0:T(8,128)(2,1)S(1)} %get-tuple-element.393), channel_id=1, source_target_pairs={{0,8},{8,16},{16,24},{24,28},{28,20},{20,12},{12,4},{4,0},{1,9},{9... | collective-permute-start | bytes 786440 | tf_op jit(solution)/shard_map/ppermute | solution.py:1155
  175.3 7.0 %collective-permute-start.45 = (bf16[1024,128]{1,0:T(8,128)(2,1)S(1)}, bf16[1024,128]{1,0:T(8,128)(2,1)S(1)}, u32[]{:S(2)}, u32[]{:S(2)}) collective-permute-start(bf16[1024,128]{1,0:T(8,128)(2,1)S(1)} %get-tuple-element.392), channel_id=1, source_target_pairs={{8,0},{16,8},{24,16},{28,24},{20,28},{12,20},{4,12},{0,4},{9,1},{1... | collective-permute-start | bytes 786440 | tf_op jit(solution)/shard_map/ppermute | solution.py:1155
  176.7 16.9 %collective-permute-start.69 = (bf16[1024,128]{1,0:T(8,128)(2,1)S(1)}, bf16[1024,128]{1,0:T(8,128)(2,1)S(1)}, u32[]{:S(2)}, u32[]{:S(2)}) collective-permute-start(bf16[1024,128]{1,0:T(8,128)(2,1)S(1)} %get-tuple-element.360), channel_id=1, source_target_pairs={{0,8},{8,16},{16,24},{24,28},{28,20},{20,12},{12,4},{4,0},{1,9},{9... | collective-permute-start | bytes 786440 | tf_op jit(solution)/shard_map/ppermute | solution.py:1155
  177.6 19.7 %collective-permute-start.70 = (bf16[1024,128]{1,0:T(8,128)(2,1)}, bf16[1024,128]{1,0:T(8,128)(2,1)}, u32[]{:S(2)}, u32[]{:S(2)}) collective-permute-start(bf16[1024,128]{1,0:T(8,128)(2,1)} %get-tuple-element.361), channel_id=1, source_target_pairs={{8,0},{16,8},{24,16},{28,24},{20,28},{12,20},{4,12},{0,4},{9,1},{1... | collective-permute-start | bytes 786440 | tf_op jit(solution)/shard_map/ppermute | solution.py:1155
  183.8 16.5 %collective-permute-start.48 = (bf16[256,1024]{1,0:T(8,128)(2,1)S(1)}, bf16[256,1024]{1,0:T(8,128)(2,1)S(1)}, u32[]{:S(2)}, u32[]{:S(2)}) collective-permute-start(bf16[256,1024]{1,0:T(8,128)(2,1)S(1)} %multiply_convert_fusion.own_ref), channel_id=1, source_target_pairs={{0,1},{1,0},{2,3},{3,2},{4,5},{5,4},{6,7},{7,6},{8,9},{9,8},{10,11... | collective-permute-start | bytes 1572872 | tf_op jit(solution)/shard_map/ppermute | solution.py:1210
  185.7 13.1 %collective-permute-start.49 = (bf16[2048,128]{1,0:T(8,128)(2,1)}, bf16[2048,128]{1,0:T(8,128)(2,1)}, u32[]{:S(2)}, u32[]{:S(2)}) collective-permute-start(bf16[2048,128]{1,0:T(8,128)(2,1)} %pad_maximum_fusion.1), channel_id=1, source_target_pairs={{0,8},{8,16},{16,24},{24,28},{28,20},{20,12},{12,4},{4,0},{1,9},{9... | collective-permute-start | bytes 1572872 | tf_op jit(solution)/shard_map/ppermute | solution.py:1155
  186.7 13.2 %collective-permute-start.50 = (bf16[2048,128]{1,0:T(8,128)(2,1)}, bf16[2048,128]{1,0:T(8,128)(2,1)}, u32[]{:S(2)}, u32[]{:S(2)}) collective-permute-start(bf16[2048,128]{1,0:T(8,128)(2,1)} %pad_maximum_fusion.2), channel_id=1, source_target_pairs={{8,0},{16,8},{24,16},{28,24},{20,28},{12,20},{4,12},{0,4},{9,1},{1... | collective-permute-start | bytes 1572872 | tf_op jit(solution)/shard_map/ppermute | solution.py:1155
  193.5 8.9 %collective-permute-start.47 = (bf16[256,1024]{1,0:T(8,128)(2,1)}, bf16[256,1024]{1,0:T(8,128)(2,1)S(1)}, u32[]{:S(2)}, u32[]{:S(2)}) collective-permute-start(bf16[256,1024]{1,0:T(8,128)(2,1)} %get-tuple-element.302), channel_id=1, source_target_pairs={{0,2},{2,0},{1,3},{3,1},{4,6},{6,4},{5,7},{7,5},{8,10},{10,8},{9,1... | collective-permute-start | bytes 1572872 | tf_op jit(solution)/shard_map/ppermute | solution.py:1220
  197.3 6.8 %collective-permute-start.46 = (bf16[256,1024]{1,0:T(8,128)(2,1)S(1)}, bf16[256,1024]{1,0:T(8,128)(2,1)S(1)}, u32[]{:S(2)}, u32[]{:S(2)}) collective-permute-start(bf16[256,1024]{1,0:T(8,128)(2,1)S(1)} %get-tuple-element.300), channel_id=1, source_target_pairs={{0,2},{2,0},{1,3},{3,1},{4,6},{6,4},{5,7},{7,5},{8,10},{10,8},{9,1... | collective-permute-start | bytes 1572872 | tf_op jit(solution)/shard_map/ppermute | solution.py:1219
  198.8 44.1 %collective-permute-start.71 = (bf16[1024,128]{1,0:T(8,128)(2,1)S(1)}, bf16[1024,128]{1,0:T(8,128)(2,1)S(1)}, u32[]{:S(2)}, u32[]{:S(2)}) collective-permute-start(bf16[1024,128]{1,0:T(8,128)(2,1)S(1)} %get-tuple-element.405), channel_id=1, source_target_pairs={{0,8},{8,16},{16,24},{24,28},{28,20},{20,12},{12,4},{4,0},{1,9},{9... | collective-permute-start | bytes 786440 | tf_op jit(solution)/shard_map/ppermute | solution.py:1155
  199.9 43.0 %collective-permute-start.72 = (bf16[1024,128]{1,0:T(8,128)(2,1)S(1)}, bf16[1024,128]{1,0:T(8,128)(2,1)S(1)}, u32[]{:S(2)}, u32[]{:S(2)}) collective-permute-start(bf16[1024,128]{1,0:T(8,128)(2,1)S(1)} %get-tuple-element.404), channel_id=1, source_target_pairs={{8,0},{16,8},{24,16},{28,24},{20,28},{12,20},{4,12},{0,4},{9,1},{1... | collective-permute-start | bytes 786440 | tf_op jit(solution)/shard_map/ppermute | solution.py:1155
  200.4 6.3 %collective-permute-start.51 = (bf16[256,1024]{1,0:T(8,128)(2,1)S(1)}, bf16[256,1024]{1,0:T(8,128)(2,1)S(1)}, u32[]{:S(2)}, u32[]{:S(2)}) collective-permute-start(bf16[256,1024]{1,0:T(8,128)(2,1)S(1)} %multiply_convert_fusion.own_ref), channel_id=1, source_target_pairs={{0,2},{2,0},{1,3},{3,1},{4,6},{6,4},{5,7},{7,5},{8,10},{10,8},{9,1... | collective-permute-start | bytes 1572872 | tf_op jit(solution)/shard_map/ppermute | solution.py:1215
  206.7 14.6 %collective-permute-start.54 = (bf16[2048,128]{1,0:T(8,128)(2,1)S(1)}, bf16[2048,128]{1,0:T(8,128)(2,1)S(1)}, u32[]{:S(2)}, u32[]{:S(2)}) collective-permute-start(bf16[2048,128]{1,0:T(8,128)(2,1)S(1)} %get-tuple-element.324), channel_id=1, source_target_pairs={{0,8},{8,16},{16,24},{24,28},{28,20},{20,12},{12,4},{4,0},{1,9},{9... | collective-permute-start | bytes 1572872 | tf_op jit(solution)/shard_map/ppermute | solution.py:1155
  207.7 13.6 %collective-permute-start.55 = (bf16[2048,128]{1,0:T(8,128)(2,1)S(1)}, bf16[2048,128]{1,0:T(8,128)(2,1)S(1)}, u32[]{:S(2)}, u32[]{:S(2)}) collective-permute-start(bf16[2048,128]{1,0:T(8,128)(2,1)S(1)} %get-tuple-element.325), channel_id=1, source_target_pairs={{8,0},{16,8},{24,16},{28,24},{20,28},{12,20},{4,12},{0,4},{9,1},{1... | collective-permute-start | bytes 1572872 | tf_op jit(solution)/shard_map/ppermute | solution.py:1155
  208.4 21.8 %collective-permute-start.53 = (bf16[256,1024]{1,0:T(8,128)(2,1)S(1)}, bf16[256,1024]{1,0:T(8,128)(2,1)S(1)}, u32[]{:S(2)}, u32[]{:S(2)}) collective-permute-start(bf16[256,1024]{1,0:T(8,128)(2,1)S(1)} %add_convert_fusion.2), channel_id=1, source_target_pairs={{0,1},{1,0},{2,3},{3,2},{4,5},{5,4},{6,7},{7,6},{8,9},{9,8},{10,11... | collective-permute-start | bytes 1572872 | tf_op jit(solution)/shard_map/ppermute | solution.py:1225
  221.6 12.2 %collective-permute-start.59 = (bf16[2048,128]{1,0:T(8,128)(2,1)S(1)}, bf16[2048,128]{1,0:T(8,128)(2,1)S(1)}, u32[]{:S(2)}, u32[]{:S(2)}) collective-permute-start(bf16[2048,128]{1,0:T(8,128)(2,1)S(1)} %get-tuple-element.339), channel_id=1, source_target_pairs={{0,8},{8,16},{16,24},{24,28},{28,20},{20,12},{12,4},{4,0},{1,9},{9... | collective-permute-start | bytes 1572872 | tf_op jit(solution)/shard_map/ppermute | solution.py:1155
  222.7 13.3 %collective-permute-start.60 = (bf16[2048,128]{1,0:T(8,128)(2,1)S(1)}, bf16[2048,128]{1,0:T(8,128)(2,1)S(1)}, u32[]{:S(2)}, u32[]{:S(2)}) collective-permute-start(bf16[2048,128]{1,0:T(8,128)(2,1)S(1)} %get-tuple-element.340), channel_id=1, source_target_pairs={{8,0},{16,8},{24,16},{28,24},{20,28},{12,20},{4,12},{0,4},{9,1},{1... | collective-permute-start | bytes 1572872 | tf_op jit(solution)/shard_map/ppermute | solution.py:1155
  230.2 7.0 %collective-permute-start.57 = (bf16[256,1024]{1,0:T(8,128)(2,1)S(1)}, bf16[256,1024]{1,0:T(8,128)(2,1)S(1)}, u32[]{:S(2)}, u32[]{:S(2)}) collective-permute-start(bf16[256,1024]{1,0:T(8,128)(2,1)S(1)} %get-tuple-element.335), channel_id=1, source_target_pairs={{0,2},{2,0},{1,3},{3,1},{4,6},{6,4},{5,7},{7,5},{8,10},{10,8},{9,1... | collective-permute-start | bytes 1572872 | tf_op jit(solution)/shard_map/ppermute | solution.py:1220
  236.0 5.2 %collective-permute-start.61 = (bf16[528,128]{1,0:T(8,128)(2,1)S(1)}, bf16[528,128]{1,0:T(8,128)(2,1)S(1)}, u32[]{:S(2)}, u32[]{:S(2)}) collective-permute-start(bf16[528,128]{1,0:T(8,128)(2,1)S(1)} %get-tuple-element.346), channel_id=1, source_target_pairs={{0,8},{8,16},{16,24},{24,28},{28,20},{20,12},{12,4},{4,0},{1,9},{9... | collective-permute-start | bytes 405512 | tf_op jit(solution)/shard_map/ppermute | solution.py:1155
  241.4 5.8 %collective-permute-start.63 = (bf16[1040,128]{1,0:T(8,128)(2,1)S(1)}, bf16[1040,128]{1,0:T(8,128)(2,1)S(1)}, u32[]{:S(2)}, u32[]{:S(2)}) collective-permute-start(bf16[1040,128]{1,0:T(8,128)(2,1)S(1)} %pad_maximum_fusion.3), channel_id=1, source_target_pairs={{0,8},{8,16},{16,24},{24,28},{28,20},{20,12},{12,4},{4,0},{1,9},{9... | collective-permute-start | bytes 798728 | tf_op jit(solution)/shard_map/ppermute | solution.py:1155
  242.3 5.6 %collective-permute-start.64 = (bf16[1040,128]{1,0:T(8,128)(2,1)S(1)}, bf16[1040,128]{1,0:T(8,128)(2,1)S(1)}, u32[]{:S(2)}, u32[]{:S(2)}) collective-permute-start(bf16[1040,128]{1,0:T(8,128)(2,1)S(1)} %pad_maximum_fusion.4), channel_id=1, source_target_pairs={{8,0},{16,8},{24,16},{28,24},{20,28},{12,20},{4,12},{0,4},{9,1},{1... | collective-permute-start | bytes 798728 | tf_op jit(solution)/shard_map/ppermute | solution.py:1155
  242.9 10.8 %collective-permute-start.58 = (bf16[256,1024]{1,0:T(8,128)(2,1)S(1)}, bf16[256,1024]{1,0:T(8,128)(2,1)S(1)}, u32[]{:S(2)}, u32[]{:S(2)}) collective-permute-start(bf16[256,1024]{1,0:T(8,128)(2,1)S(1)} %add_convert_fusion), channel_id=1, source_target_pairs={{0,1},{1,0},{2,3},{3,2},{4,5},{5,4},{6,7},{7,6},{8,9},{9,8},{10,11... | collective-permute-start | bytes 1572872 | tf_op jit(solution)/shard_map/ppermute | solution.py:1225
  248.0 7.5 %collective-permute-start.65 = (bf16[1040,128]{1,0:T(8,128)(2,1)S(1)}, bf16[1040,128]{1,0:T(8,128)(2,1)S(1)}, u32[]{:S(2)}, u32[]{:S(2)}) collective-permute-start(bf16[1040,128]{1,0:T(8,128)(2,1)S(1)} %get-tuple-element.399), channel_id=1, source_target_pairs={{0,8},{8,16},{16,24},{24,28},{28,20},{20,12},{12,4},{4,0},{1,9},{9... | collective-permute-start | bytes 798728 | tf_op jit(solution)/shard_map/ppermute | solution.py:1155
  249.5 6.0 %collective-permute-start.66 = (bf16[1040,128]{1,0:T(8,128)(2,1)S(1)}, bf16[1040,128]{1,0:T(8,128)(2,1)S(1)}, u32[]{:S(2)}, u32[]{:S(2)}) collective-permute-start(bf16[1040,128]{1,0:T(8,128)(2,1)S(1)} %get-tuple-element.398), channel_id=1, source_target_pairs={{8,0},{16,8},{24,16},{28,24},{20,28},{12,20},{4,12},{0,4},{9,1},{1... | collective-permute-start | bytes 798728 | tf_op jit(solution)/shard_map/ppermute | solution.py:1155
  255.6 5.3 %collective-permute-start.67 = (bf16[1040,128]{1,0:T(8,128)(2,1)S(1)}, bf16[1040,128]{1,0:T(8,128)(2,1)S(1)}, u32[]{:S(2)}, u32[]{:S(2)}) collective-permute-start(bf16[1040,128]{1,0:T(8,128)(2,1)S(1)} %get-tuple-element.356), channel_id=1, source_target_pairs={{0,8},{8,16},{16,24},{24,28},{28,20},{20,12},{12,4},{4,0},{1,9},{9... | collective-permute-start | bytes 798728 | tf_op jit(solution)/shard_map/ppermute | solution.py:1155
  257.1 5.3 %collective-permute-start.68 = (bf16[1040,128]{1,0:T(8,128)(2,1)S(1)}, bf16[1040,128]{1,0:T(8,128)(2,1)S(1)}, u32[]{:S(2)}, u32[]{:S(2)}) collective-permute-start(bf16[1040,128]{1,0:T(8,128)(2,1)S(1)} %get-tuple-element.357), channel_id=1, source_target_pairs={{8,0},{16,8},{24,16},{28,24},{20,28},{12,20},{4,12},{0,4},{9,1},{1... | collective-permute-start | bytes 798728 | tf_op jit(solution)/shard_map/ppermute | solution.py:1155
  (61 other events, 914.0 us)
where the time goes:
time: 314 us; the launch traced here: 308 us
  waiting for transfers between devices  92.4 us (29%)
  Pallas kernels  73.7 us (23%)
  starting transfers between devices  73.5 us (23%)
  blocking collectives  38.5 us (12%)
  other arithmetic  21.5 us (7%)
  local copies, waits for them, and re-layouts  6.8 us (2%)
    all_to_all x1, blocking collectives, fast_body(): lax.all_to_all(pieces, EVERY, split_axis=0, concat_axis=0, tiled=True)  38.5 us
    ppermute x24, waiting for transfers between devices, both_ways(): lax.ppermute(ahead, GROUP, AHEAD)  36 us
    all_to_all x1, waiting for transfers between devices, fast_body(): lax.all_to_all(pieces, EVERY, split_axis=0, concat_axis=0, tiled=True)  28.2 us
    ppermute x24, starting transfers between devices, both_ways(): lax.ppermute(back, GROUP, BACK)  21.1 us
    ppermute x24, starting transfers between devices, both_ways(): lax.ppermute(ahead, GROUP, AHEAD)  15.9 us
    pallas_call x1, Pallas kernels, attention_back(): pl.pallas_call(attend_back_kernel, out_shape=(jax.ShapeDtypeStruct((1024,...  11.7 us
    ppermute x3, starting transfers between devices, half_sum(): kept = near + lax.ppermute(far, 'c', SWAP).astype(jnp.float32)  11.2 us
    pallas_call x1, Pallas kernels, front(): pl.pallas_call(front_kernel, out_shape=(pltpu.HBM((1024, D), jnp.bfloat16...  10.6 us
  transfers between devices with their start and end apart: 74, of which 27 were waited for; matrix products, arithmetic and copies ran while one was open for 6% of the time, Pallas kernels for 22%

commit v1 on v0

--- a/solution.py
+++ b/solution.py
@@ -392,7 +392,7 @@
 
         lax.fori_loop(0, LINES // 64, body, 0, unroll=4)
 
-    tail_ref[...] = shifted(LINES // 64)
+    tail_ref[:TAIL, :] = shifted(LINES // 64)
     for kind in range(3):
 
         @pl.when(is_kind(me, kind))
@@ -439,8 +439,8 @@
         ],
         out_specs=pl.BlockSpec(memory_space=pltpu.VMEM),
         scratch_shapes=[
-            pltpu.VMEM((LINES // 64 * PITCH, 128), jnp.float32),
-            pltpu.VMEM((TAIL, 128), jnp.float32),
+            pltpu.VMEM((LINES // 64 * PITCH + PITCH, 128), jnp.float32),
+            pltpu.VMEM((TAIL + 16, 128), jnp.float32),
         ],
         compiler_params=vmem(12),
         name="spread",
@@ -512,7 +512,7 @@
         out_specs=pl.BlockSpec(memory_space=pltpu.VMEM),
         scratch_shapes=[
             pltpu.VMEM((LINES + TAIL, 128), jnp.float32),
-            pltpu.VMEM((32 * 136, 128), jnp.float32),
+            pltpu.VMEM((33 * 136, 128), jnp.float32),
         ],
         compiler_params=vmem(12),
         name="collect",

time: 314 us -> 314 us (level)
  no operation moved by 1% of the time
where the time goes in v1:
time: 314 us; the launch traced here: 308 us
  waiting for transfers between devices  92.4 us (29%)
  Pallas kernels  73.7 us (23%)
  starting transfers between devices  73.5 us (23%)
  blocking collectives  38.5 us (12%)
  other arithmetic  21.5 us (7%)
  local copies, waits for them, and re-layouts  6.8 us (2%)
    all_to_all x1, blocking collectives, fast_body(): lax.all_to_all(pieces, EVERY, split_axis=0, concat_axis=0, tiled=True)  38.5 us
    ppermute x24, waiting for transfers between devices, both_ways(): lax.ppermute(ahead, GROUP, AHEAD)  36 us
    all_to_all x1, waiting for transfers between devices, fast_body(): lax.all_to_all(pieces, EVERY, split_axis=0, concat_axis=0, tiled=True)  28.2 us
    ppermute x24, starting transfers between devices, both_ways(): lax.ppermute(back, GROUP, BACK)  21.1 us
    ppermute x24, starting transfers between devices, both_ways(): lax.ppermute(ahead, GROUP, AHEAD)  15.9 us
    pallas_call x1, Pallas kernels, attention_back(): pl.pallas_call(attend_back_kernel, out_shape=(jax.ShapeDtypeStruct((1024,...  11.7 us
    ppermute x3, starting transfers between devices, half_sum(): kept = near + lax.ppermute(far, 'c', SWAP).astype(jnp.float32)  11.2 us
    pallas_call x1, Pallas kernels, front(): pl.pallas_call(front_kernel, out_shape=(pltpu.HBM((1024, D), jnp.bfloat16...  10.6 us
  transfers between devices with their start and end apart: 74, of which 27 were waited for; matrix products, arithmetic and copies ran while one was open for 6% of the time, Pallas kernels for 22%

profile of v1, /device:TPU:1, one launch (start us, length us, event | category | flops | bytes accessed | tf_op | source)
XLA Modules:
  0.0 308.4 jit_solution(12307403963875344318)
XLA Ops:
  0.6 1.7 pad_bitcast_fusion.flat_ref
  2.4 3.6 %spread.1 = bf16[32,144,128]{2,1,0:T(8,128)(2,1)} custom-call(s32[1]{0:T(128)} %bitcast.1.me_ref.y_ref, f32[4224,128]{1,0:T(8,128)S(1)} %pad_bitcast_fusion.flat_ref), custom_call_target="tpu_custom_call" | custom-call | tf_op jit(solution)/shard_map/spread/pallas_call | solution.py:433
  6.0 7.2 %all-to-all-start = ((bf16[32,144,128]{2,1,0:T(8,128)(2,1)}), bf16[32,144,128]{2,1,0:T(8,128)(2,1)S(1)}, u32[]{:S(2)}, u32[]{:S(2)}) async-start(bf16[32,144,128]{2,1,0:T(8,128)(2,1)} %spread.1), calls=%async_computation | async-start | bytes 2359296 | tf_op jit(solution)/shard_map/all_to_all | solution.py:1254
  13.6 28.2 %all-to-all-done.piece_ref = bf16[32,144,128]{2,1,0:T(8,128)(2,1)S(1)} async-done(((bf16[32,144,128]{2,1,0:T(8,128)(2,1)}), bf16[32,144,128]{2,1,0:T(8,128)(2,1)S(1)}, u32[]{:S(2)}, u32[]{:S(2)}) %all-to-all-start) | async-done | bytes 1179680 | tf_op jit(solution)/shard_map/all_to_all | solution.py:1254
  41.9 1.8 collective-permute-start
  44.7 1.9 fusion.23
  46.6 3.3 %collective-permute-done.refs_1_ = bf16[1040,128]{1,0:T(8,128)(2,1)S(1)} collective-permute-done((bf16[1040,128]{1,0:T(8,128)(2,1)S(1)}, bf16[1040,128]{1,0:T(8,128)(2,1)S(1)}, u32[]{:S(2)}, u32[]{:S(2)}) %collective-permute-start) | collective-permute-done | bytes 266272 | tf_op jit(solution)/shard_map/ppermute | solution.py:1155
  49.9 2.0 collective-permute-done.1.refs_2_
  51.9 1.5 collective-permute-start.4
  53.4 6.5 %collective-permute-done.3.refs_3_ = bf16[1040,128]{1,0:T(8,128)(2,1)S(1)} collective-permute-done((bf16[1040,128]{1,0:T(8,128)(2,1)S(1)}, bf16[1040,128]{1,0:T(8,128)(2,1)S(1)}, u32[]{:S(2)}, u32[]{:S(2)}) %collective-permute-start.3) | collective-permute-done | bytes 266272 | tf_op jit(solution)/shard_map/ppermute | solution.py:1155
  59.9 1.5 collective-permute-start.7
  61.3 1.4 collective-permute-start.8
  62.8 4.2 %collective-permute-done.6.refs_5_ = bf16[1040,128]{1,0:T(8,128)(2,1)S(1)} collective-permute-done((bf16[1040,128]{1,0:T(8,128)(2,1)S(1)}, bf16[1040,128]{1,0:T(8,128)(2,1)S(1)}, u32[]{:S(2)}, u32[]{:S(2)}) %collective-permute-start.6) | collective-permute-done | bytes 266272 | tf_op jit(solution)/shard_map/ppermute | solution.py:1155
  70.5 7.7 %collective-permute-done.12 = bf16[2048,128]{1,0:T(8,128)(2,1)S(1)} collective-permute-done((bf16[2048,128]{1,0:T(8,128)(2,1)S(1)}, bf16[2048,128]{1,0:T(8,128)(2,1)S(1)}, u32[]{:S(2)}, u32[]{:S(2)}) %collective-permute-start.12) | collective-permute-done | bytes 524320 | tf_op jit(solution)/shard_map/ppermute | solution.py:1155
  78.3 1.9 collective-permute-done.11.refs_8_
  81.7 1.6 collective-permute-start.16
  83.4 10.6 %front.1 = (bf16[1024,1024]{1,0:T(8,128)(2,1)}, bf16[1024,768]{1,0:T(8,128)(2,1)}, bf16[1024,768]{1,0:T(8,128)(2,1)}, bf16[1024,256]{1,0:T(8,128)(2,1)S(1)}, f32[1024,4]{1,0:T(8,128)}) custom-call(bf16[1024,1024]{1,0:T(8,128)(2,1)S(1)} %get-tuple-element.217.x_ref, f32[1024,1]{1,0:T(8,128)S(1)} %get-tuple-element.218.mean_ref, ...), custom_call_target="tpu_custom_call" | custom-call | flops 12884901888 | bytes 8388608 | tf_op jit(solution)/shard_map/front/pallas_call | solution.py:806
  94.1 3.6 %collective-permute-start.19 = (bf16[8,256,128]{2,1,0:T(8,128)(2,1)S(1)}, bf16[8,256,128]{2,1,0:T(8,128)(2,1)S(1)}, u32[]{:S(2)}, u32[]{:S(2)}) collective-permute-start(bf16[8,256,128]{2,1,0:T(8,128)(2,1)S(1)} %get-tuple-element.228.refs_0_.ring_ref), channel_id=1, source_target_pairs={{0,2},{2,0},{1,3},{3,1},{4,6},{6,4},{5,7},{7,5},{8,10},{10,8},{9,1... | collective-permute-start | bytes 1572872 | tf_op jit(solution)/shard_map/ppermute | solution.py:1215
  97.7 1.7 collective-permute-start.18
  99.5 1.4 collective-permute-start.24
  101.5 9.8 %collective-permute-done.18.pair_ref = bf16[1024,256]{1,0:T(8,128)(2,1)S(1)} collective-permute-done((bf16[1024,256]{1,0:T(8,128)(2,1)S(1)}, bf16[1024,256]{1,0:T(8,128)(2,1)S(1)}, u32[]{:S(2)}, u32[]{:S(2)}) %collective-permute-start.18) | collective-permute-done | bytes 524320 | tf_op jit(solution)/shard_map/ppermute | solution.py:1210
  112.6 1.3 collective-permute-done.21.far_ref
  114.7 1.4 collective-permute-start.26
  117.6 1.8 collective-permute-start.28
  119.5 3.3 %mix.1 = (bf16[1024,1024]{1,0:T(8,128)(2,1)S(1)}, f32[512,1024]{1,0:T(8,128)S(1)}) custom-call(bf16[1024,1024]{1,0:T(8,128)(2,1)S(1)} %get-tuple-element.217.x_ref, bf16[1024,256]{1,0:T(8,128)(2,1)S(1)} %get-tuple-element.230.own_ref.attn_ref, bf16[1024,256]{1,0:T(8,128)(2,1)S(1)} %collective-permute-done.18.pair_ref, ...), custom_call_target="tpu_custom_call" | custom-call | flops 3221225472 | bytes 10485760 | tf_op jit(solution)/shard_map/mix/pallas_call | solution.py:844
  122.8 1.3 copy-done.24
  124.1 1.5 collective-permute-start.31
  126.4 1.5 collective-permute-done.27
  128.7 2.6 join_gate_up.1
  131.6 4.5 %gate.1 = (f32[4,1024,512]{2,1,0:T(8,128)S(1)}, bf16[1024,1024]{1,0:T(8,128)(2,1)S(1)}) custom-call(bf16[1024,1024]{1,0:T(8,128)(2,1)S(1)} %copy-done.25, bf16[4,1024,512]{2,1,0:T(8,128)(2,1)S(1)} %bitcast.127), custom_call_target="tpu_custom_call" | custom-call | flops 5368709120 | bytes 16777216 | tf_op jit(solution)/shard_map/gate/pallas_call | solution.py:871
  137.6 3.9 %down_grad.1 = (bf16[8,1024,128]{2,1,0:T(8,128)(2,1)S(1)}, bf16[1024,1024]{1,0:T(8,128)(2,1)S(1)}) custom-call(s32[1]{0:T(128)} %bitcast.1.me_ref.y_ref, bf16[1024,1024]{1,0:T(8,128)(2,1)S(1)} %get-tuple-element.298.hidden_ref, bf16[256,1024]{1,0:T(8,128)(2,1)S(1)} %bitcast.131, bf16[256,1024]{1,0:T(8,128)(2,1)} %collective-permute-done.14.pair_ref, ...), custom_call_target="tpu_custom_call" | custom-call | flops 3221225472 | bytes 8388608 | tf_op jit(solution)/shard_map/down_grad/pallas_call | solution.py:900
  143.2 1.2 collective-permute-start.36
  144.6 1.7 join_down.1._
  147.3 1.5 collective-permute-start.38
  149.1 3.8 %hidden_back.1.d_both_ref = bf16[4,1024,512]{2,1,0:T(8,128)(2,1)S(1)} custom-call(f32[4,1024,512]{2,1,0:T(8,128)S(1)} %get-tuple-element.253.gate_up_ref, bf16[1024,1024]{1,0:T(8,128)(2,1)S(1)} %get-tuple-element.261.d_mlp_ref, bf16[1024,1024]{1,0:T(8,128)(2,1)S(1)} %join_down_rest.1.w_ref), custom_call_target="tpu_custom_call" | custom-call | flops 4294967296 | bytes 18874368 | tf_op jit(solution)/shard_map/hidden_back/pallas_call | solution.py:943
  153.2 1.3 collective-permute-start.40
  154.5 4.9 %norm_back.1 = (f32[256,1024]{1,0:T(8,128)S(1)}, f32[256,1024]{1,0:T(8,128)S(1)}, bf16[256,1024]{1,0:T(8,128)(2,1)S(1)}, bf16[256,1024]{1,0:T(8,128)(2,1)S(1)}) custom-call(s32[1]{0:T(128)} %bitcast.1.me_ref.y_ref, bf16[4,1024,512]{2,1,0:T(8,128)(2,1)S(1)} %hidden_back.1.d_both_ref, bf16[4,1024,512]{2,1,0:T(8,128)(2,1)S(1)} %bitcast.128), custom_call_target="tpu_custom_call" | custom-call | flops 5368709120 | bytes 12582912 | tf_op jit(solution)/shard_map/norm_back/pallas_call | solution.py:965
  159.5 5.5 %collective-permute-start.42 = (bf16[256,1024]{1,0:T(8,128)(2,1)S(1)}, bf16[256,1024]{1,0:T(8,128)(2,1)S(1)}, u32[]{:S(2)}, u32[]{:S(2)}) collective-permute-start(bf16[256,1024]{1,0:T(8,128)(2,1)S(1)} %get-tuple-element.290), channel_id=1, source_target_pairs={{0,2},{2,0},{1,3},{3,1},{4,6},{6,4},{5,7},{7,5},{8,10},{10,8},{9,1... | collective-permute-start | bytes 1572872 | tf_op jit(solution)/shard_map/ppermute | solution.py:1220
  167.6 1.5 collective-permute-start.43
  169.1 4.5 %gate_grad.1 = bf16[8,2048,128]{2,1,0:T(8,128)(2,1)S(1)} custom-call(bf16[1024,1024]{1,0:T(8,128)(2,1)S(1)} %copy-done.25, bf16[4,1024,512]{2,1,0:T(8,128)(2,1)S(1)} %hidden_back.1.d_both_ref), custom_call_target="tpu_custom_call" | custom-call | flops 5368709120 | bytes 10485760 | tf_op jit(solution)/shard_map/gate_grad/pallas_call | solution.py:991
  173.8 1.5 collective-permute-start.44
  178.3 3.4 %collective-permute-done.44 = bf16[1024,128]{1,0:T(8,128)(2,1)S(1)} collective-permute-done((bf16[1024,128]{1,0:T(8,128)(2,1)S(1)}, bf16[1024,128]{1,0:T(8,128)(2,1)S(1)}, u32[]{:S(2)}, u32[]{:S(2)}) %collective-permute-start.44) | collective-permute-done | bytes 262176 | tf_op jit(solution)/shard_map/ppermute | solution.py:1155
  187.2 6.3 %out.1 = (f32[256,1024]{1,0:T(8,128)}, f32[256,1024]{1,0:T(8,128)}, bf16[256,1024]{1,0:T(8,128)(2,1)S(1)}, bf16[256,1024]{1,0:T(8,128)(2,1)}, f32[1,1024]{1,0:T(1,128)S(1)}) custom-call(s32[1]{0:T(128)} %bitcast.1.me_ref.y_ref, bf16[1024,1024]{1,0:T(8,128)(2,1)S(1)} %get-tuple-element.298.hidden_ref, bf16[1024,1024]{1,0:T(8,128)(2,1)S(1)} %join_down_rest.1.w_ref, ...), custom_call_target="tpu_custom_call" | custom-call | flops 3221225472 | bytes 10485760 | tf_op jit(solution)/shard_map/out/pallas_call | solution.py:1019
  193.5 3.7 %collective-permute-start.47 = (bf16[256,1024]{1,0:T(8,128)(2,1)}, bf16[256,1024]{1,0:T(8,128)(2,1)S(1)}, u32[]{:S(2)}, u32[]{:S(2)}) collective-permute-start(bf16[256,1024]{1,0:T(8,128)(2,1)} %get-tuple-element.302), channel_id=1, source_target_pairs={{0,2},{2,0},{1,3},{3,1},{4,6},{6,4},{5,7},{7,5},{8,10},{10,8},{9,1... | collective-permute-start | bytes 1572872 | tf_op jit(solution)/shard_map/ppermute | solution.py:1220
  197.4 1.4 fusion.24
  200.4 2.1 collective-permute-start.51
  202.5 1.5 convert_add_fusion.7
  205.0 1.6 fusion.15
  209.6 11.7 %attend_back.1 = (bf16[1024,768]{1,0:T(8,128)(2,1)S(1)}, bf16[8,256,128]{2,1,0:T(8,128)(2,1)S(1)}) custom-call(s32[1]{0:T(128)} %bitcast.1.me_ref.y_ref, bf16[256,1024]{1,0:T(8,128)(2,1)S(1)} %multiply_convert_fusion.own_ref, bf16[256,1024]{1,0:T(8,128)(2,1)S(1)} %collective-permute-done.48.pair_ref, bf16[256,1024]{1,0:T(8,128)(2,1)S(1)} %collective-permute-done.51.far_ref, ...), custom_call_target="tpu_custom_call" | custom-call | flops 12884901888 | bytes 10485760 | tf_op jit(solution)/shard_map/attend_back/pallas_call | solution.py:1084
  221.6 1.1 collective-permute-start.59
  223.3 6.9 %grad.1 = (bf16[8,1040,128]{2,1,0:T(8,128)(2,1)S(1)}, f32[256,1024]{1,0:T(8,128)S(1)}, f32[256,1024]{1,0:T(8,128)S(1)}, bf16[256,1024]{1,0:T(8,128)(2,1)S(1)}, bf16[256,1024]{1,0:T(8,128)(2,1)S(1)}) custom-call(s32[1]{0:T(128)} %bitcast.1.me_ref.y_ref, bf16[1024,1024]{1,0:T(8,128)(2,1)S(1)} %copy-done.26, bf16[1024,768]{1,0:T(8,128)(2,1)S(1)} %copy-done.27, ...), custom_call_target="tpu_custom_call" | custom-call | flops 8589934592 | bytes 12582912 | tf_op jit(solution)/shard_map/grad/pallas_call | solution.py:1136
  230.2 1.9 collective-permute-start.57
  233.8 2.2 collective-permute-start.56
  237.9 3.3 %collective-permute-done.62 = bf16[512,128]{1,0:T(8,128)(2,1)S(1)} collective-permute-done((bf16[512,128]{1,0:T(8,128)(2,1)S(1)}, bf16[512,128]{1,0:T(8,128)(2,1)S(1)}, u32[]{:S(2)}, u32[]{:S(2)}) %collective-permute-start.62) | collective-permute-done | bytes 131104 | tf_op jit(solution)/shard_map/ppermute | solution.py:1155
  244.5 2.7 collective-permute-done.63
  248.0 1.5 collective-permute-start.65
  249.5 4.2 %collective-permute-done.58 = bf16[256,1024]{1,0:T(8,128)(2,1)S(1)} collective-permute-done((bf16[256,1024]{1,0:T(8,128)(2,1)S(1)}, bf16[256,1024]{1,0:T(8,128)(2,1)S(1)}, u32[]{:S(2)}, u32[]{:S(2)}) %collective-permute-start.58) | collective-permute-done | bytes 524320 | tf_op jit(solution)/shard_map/ppermute | solution.py:1225
  254.2 1.3 fusion.9
  255.6 1.5 collective-permute-start.67
  257.4 3.6 %collective-permute-done.67 = bf16[1040,128]{1,0:T(8,128)(2,1)S(1)} collective-permute-done((bf16[1040,128]{1,0:T(8,128)(2,1)S(1)}, bf16[1040,128]{1,0:T(8,128)(2,1)S(1)}, u32[]{:S(2)}, u32[]{:S(2)}) %collective-permute-start.67) | collective-permute-done | bytes 266272 | tf_op jit(solution)/shard_map/ppermute | solution.py:1155
  260.9 1.4 collective-permute-done.68
  262.8 38.5 %all_to_all.10.piece_ref = bf16[32,144,128]{2,1,0:T(8,128)(2,1)S(1)} all-to-all(bf16[32,144,128]{2,1,0:T(8,128)(2,1)S(1)} %maximum_maximum_fusion), channel_id=1, replica_groups=mesh['z'=4,'x'=2,'c'=2,'y'=2] {'z','x','c','y'}, dimensions={0} | all-to-all | bytes 2359296 | tf_op jit(solution)/shard_map/all_to_all | solution.py:1373
  301.3 2.9 collect.1
  304.2 4.0 %multiply_subtract_fusion = (f32[524480]{0:T(1024)}, f32[524480]{0:T(1024)}, f32[524480]{0:T(1024)}, f32[524480]{0:T(1024)}) fusion(f32[524480]{0:T(1024)S(1)} %copy-done.34, f32[524480]{0:T(1024)S(1)} %copy-done.35, f32[524480]{0:T(1024)S(1)} %copy-done.36, f32[525312]{0:T(1024)S(1)} %bitcast.126), kind=kLoop, calls=%fused_computation.3 | loop fusion | flops 7867200 | bytes 16783360 | tf_op jit(solution)/shard_map/sub | solution.py:141
  (270 shorter events, 43.8 us)
Async XLA Ops:
  6.0 35.8 %all-to-all-start = ((bf16[32,144,128]{2,1,0:T(8,128)(2,1)}), bf16[32,144,128]{2,1,0:T(8,128)(2,1)S(1)}, u32[]{:S(2)}, u32[]{:S(2)}) async-start(bf16[32,144,128]{2,1,0:T(8,128)(2,1)} %spread.1), calls=%async_computation | async-start | bytes 2359296 | tf_op jit(solution)/shard_map/all_to_all | solution.py:1254
  13.3 30.6 %collective-permute-start.2 = (s32[1,2]{1,0:T(1,128)S(1)}, s32[1,2]{1,0:T(1,128)S(1)}, u32[]{:S(2)}, u32[]{:S(2)}) collective-permute-start(s32[1,2]{1,0:T(1,128)S(1)} %copy-done.13), channel_id=1, source_target_pairs={{0,2},{2,0},{1,3},{3,1},{4,6},{6,4},{5,7},{7,5},{8,10},{10,8},{9,1... | collective-permute-start | bytes 32 | tf_op jit(solution)/shard_map/ppermute | solution.py:1247
  41.9 8.0 %collective-permute-start = (bf16[1040,128]{1,0:T(8,128)(2,1)S(1)}, bf16[1040,128]{1,0:T(8,128)(2,1)S(1)}, u32[]{:S(2)}, u32[]{:S(2)}) collective-permute-start(bf16[1040,128]{1,0:T(8,128)(2,1)S(1)} %get-tuple-element.188.refs_0_), channel_id=1, source_target_pairs={{0,8},{8,16},{16,24},{24,28},{28,20},{20,12},{12,4},{4,0},{1,9},{9... | collective-permute-start | bytes 798728 | tf_op jit(solution)/shard_map/ppermute | solution.py:1155
  43.8 8.1 %collective-permute-start.1 = (bf16[1040,128]{1,0:T(8,128)(2,1)S(1)}, bf16[1040,128]{1,0:T(8,128)(2,1)S(1)}, u32[]{:S(2)}, u32[]{:S(2)}) collective-permute-start(bf16[1040,128]{1,0:T(8,128)(2,1)S(1)} %get-tuple-element.188.refs_0_), channel_id=1, source_target_pairs={{8,0},{16,8},{24,16},{28,24},{20,28},{12,20},{4,12},{0,4},{9,1},{1... | collective-permute-start | bytes 798728 | tf_op jit(solution)/shard_map/ppermute | solution.py:1155
  44.1 15.8 %collective-permute-start.5 = (bf16[256,1024]{1,0:T(8,128)(2,1)S(1)}, bf16[256,1024]{1,0:T(8,128)(2,1)S(1)}, u32[]{:S(2)}, u32[]{:S(2)}) collective-permute-start(bf16[256,1024]{1,0:T(8,128)(2,1)S(1)} %bitcast.123), channel_id=1, source_target_pairs={{0,1},{1,0},{2,3},{3,2},{4,5},{5,4},{6,7},{7,6},{8,9},{9,8},{10,11... | collective-permute-start | bytes 1572872 | tf_op jit(solution)/shard_map/ppermute | solution.py:1210
  51.9 8.0 %collective-permute-start.3 = (bf16[1040,128]{1,0:T(8,128)(2,1)S(1)}, bf16[1040,128]{1,0:T(8,128)(2,1)S(1)}, u32[]{:S(2)}, u32[]{:S(2)}) collective-permute-start(bf16[1040,128]{1,0:T(8,128)(2,1)S(1)} %collective-permute-done.refs_1_), channel_id=1, source_target_pairs={{0,8},{8,16},{16,24},{24,28},{28,20},{20,12},{12,4},{4,0},{1,9},{9... | collective-permute-start | bytes 798728 | tf_op jit(solution)/shard_map/ppermute | solution.py:1155
  51.9 8.0 %collective-permute-start.4 = (bf16[1040,128]{1,0:T(8,128)(2,1)S(1)}, bf16[1040,128]{1,0:T(8,128)(2,1)S(1)}, u32[]{:S(2)}, u32[]{:S(2)}) collective-permute-start(bf16[1040,128]{1,0:T(8,128)(2,1)S(1)} %collective-permute-done.1.refs_2_), channel_id=1, source_target_pairs={{8,0},{16,8},{24,16},{28,24},{20,28},{12,20},{4,12},{0,4},{9,1},{1... | collective-permute-start | bytes 798728 | tf_op jit(solution)/shard_map/ppermute | solution.py:1155
  59.9 7.0 %collective-permute-start.6 = (bf16[1040,128]{1,0:T(8,128)(2,1)S(1)}, bf16[1040,128]{1,0:T(8,128)(2,1)S(1)}, u32[]{:S(2)}, u32[]{:S(2)}) collective-permute-start(bf16[1040,128]{1,0:T(8,128)(2,1)S(1)} %collective-permute-done.3.refs_3_), channel_id=1, source_target_pairs={{0,8},{8,16},{16,24},{24,28},{28,20},{20,12},{12,4},{4,0},{1,9},{9... | collective-permute-start | bytes 798728 | tf_op jit(solution)/shard_map/ppermute | solution.py:1155
  59.9 7.8 %collective-permute-start.7 = (bf16[1040,128]{1,0:T(8,128)(2,1)S(1)}, bf16[1040,128]{1,0:T(8,128)(2,1)S(1)}, u32[]{:S(2)}, u32[]{:S(2)}) collective-permute-start(bf16[1040,128]{1,0:T(8,128)(2,1)S(1)} %collective-permute-done.4.refs_4_), channel_id=1, source_target_pairs={{8,0},{16,8},{24,16},{28,24},{20,28},{12,20},{4,12},{0,4},{9,1},{1... | collective-permute-start | bytes 798728 | tf_op jit(solution)/shard_map/ppermute | solution.py:1155
  61.3 6.5 %collective-permute-start.8 = (bf16[256,1024]{1,0:T(8,128)(2,1)S(1)}, bf16[256,1024]{1,0:T(8,128)(2,1)S(1)}, u32[]{:S(2)}, u32[]{:S(2)}) collective-permute-start(bf16[256,1024]{1,0:T(8,128)(2,1)S(1)} %bitcast.124), channel_id=1, source_target_pairs={{0,2},{2,0},{1,3},{3,1},{4,6},{6,4},{5,7},{7,5},{8,10},{10,8},{9,1... | collective-permute-start | bytes 1572872 | tf_op jit(solution)/shard_map/ppermute | solution.py:1215
  62.7 15.5 %collective-permute-start.12 = (bf16[2048,128]{1,0:T(8,128)(2,1)S(1)}, bf16[2048,128]{1,0:T(8,128)(2,1)S(1)}, u32[]{:S(2)}, u32[]{:S(2)}) collective-permute-start(bf16[2048,128]{1,0:T(8,128)(2,1)S(1)} %get-tuple-element.213), channel_id=1, source_target_pairs={{0,8},{8,16},{16,24},{24,28},{28,20},{20,12},{12,4},{4,0},{1,9},{9... | collective-permute-start | bytes 1572872 | tf_op jit(solution)/shard_map/ppermute | solution.py:1155
  66.9 11.3 %collective-permute-start.13 = (bf16[2048,128]{1,0:T(8,128)(2,1)S(1)}, bf16[2048,128]{1,0:T(8,128)(2,1)S(1)}, u32[]{:S(2)}, u32[]{:S(2)}) collective-permute-start(bf16[2048,128]{1,0:T(8,128)(2,1)S(1)} %get-tuple-element.213), channel_id=1, source_target_pairs={{8,0},{16,8},{24,16},{28,24},{20,28},{12,20},{4,12},{0,4},{9,1},{1... | collective-permute-start | bytes 1572872 | tf_op jit(solution)/shard_map/ppermute | solution.py:1155
  67.7 13.9 %collective-permute-start.14 = (bf16[256,1024]{1,0:T(8,128)(2,1)S(1)}, bf16[256,1024]{1,0:T(8,128)(2,1)}, u32[]{:S(2)}, u32[]{:S(2)}) collective-permute-start(bf16[256,1024]{1,0:T(8,128)(2,1)S(1)} %bitcast.129), channel_id=1, source_target_pairs={{0,1},{1,0},{2,3},{3,2},{4,5},{5,4},{6,7},{7,6},{8,9},{9,8},{10,11... | collective-permute-start | bytes 1572872 | tf_op jit(solution)/shard_map/ppermute | solution.py:1210
  69.0 12.2 %collective-permute-start.10 = (bf16[528,128]{1,0:T(8,128)(2,1)S(1)}, bf16[528,128]{1,0:T(8,128)(2,1)S(1)}, u32[]{:S(2)}, u32[]{:S(2)}) collective-permute-start(bf16[528,128]{1,0:T(8,128)(2,1)S(1)} %slice.64), channel_id=1, source_target_pairs={{0,8},{8,16},{16,24},{24,28},{28,20},{20,12},{12,4},{4,0},{1,9},{9... | collective-permute-start | bytes 405512 | tf_op jit(solution)/shard_map/ppermute | solution.py:1155
  69.7 10.4 %collective-permute-start.11 = (bf16[512,128]{1,0:T(8,128)(2,1)S(1)}, bf16[512,128]{1,0:T(8,128)(2,1)S(1)}, u32[]{:S(2)}, u32[]{:S(2)}) collective-permute-start(bf16[512,128]{1,0:T(8,128)(2,1)S(1)} %slice.65), channel_id=1, source_target_pairs={{8,0},{16,8},{24,16},{28,24},{20,28},{12,20},{4,12},{0,4},{9,1},{1... | collective-permute-start | bytes 393224 | tf_op jit(solution)/shard_map/ppermute | solution.py:1155
  81.7 12.4 %collective-permute-start.15 = (bf16[2048,128]{1,0:T(8,128)(2,1)S(1)}, bf16[2048,128]{1,0:T(8,128)(2,1)S(1)}, u32[]{:S(2)}, u32[]{:S(2)}) collective-permute-start(bf16[2048,128]{1,0:T(8,128)(2,1)S(1)} %collective-permute-done.12), channel_id=1, source_target_pairs={{0,8},{8,16},{16,24},{24,28},{28,20},{20,12},{12,4},{4,0},{1,9},{9... | collective-permute-start | bytes 1572872 | tf_op jit(solution)/shard_map/ppermute | solution.py:1155
  81.7 12.4 %collective-permute-start.16 = (bf16[2048,128]{1,0:T(8,128)(2,1)S(1)}, bf16[2048,128]{1,0:T(8,128)(2,1)S(1)}, u32[]{:S(2)}, u32[]{:S(2)}) collective-permute-start(bf16[2048,128]{1,0:T(8,128)(2,1)S(1)} %collective-permute-done.13), channel_id=1, source_target_pairs={{8,0},{16,8},{24,16},{28,24},{20,28},{12,20},{4,12},{0,4},{9,1},{1... | collective-permute-start | bytes 1572872 | tf_op jit(solution)/shard_map/ppermute | solution.py:1155
  83.4 10.8 %collective-permute-start.17 = (bf16[8,256,128]{2,1,0:T(8,128)(2,1)S(1)}, bf16[8,256,128]{2,1,0:T(8,128)(2,1)S(1)}, u32[]{:S(2)}, u32[]{:S(2)}) collective-permute-start(bf16[8,256,128]{2,1,0:T(8,128)(2,1)S(1)} %get-tuple-element.228.refs_0_.ring_ref), channel_id=1, source_target_pairs={{0,1},{1,0},{2,3},{3,2},{4,5},{5,4},{6,7},{7,6},{8,9},{9,8},{10,11... | collective-permute-start | bytes 1572872 | tf_op jit(solution)/shard_map/ppermute | solution.py:1210
  94.1 6.8 %collective-permute-start.19 = (bf16[8,256,128]{2,1,0:T(8,128)(2,1)S(1)}, bf16[8,256,128]{2,1,0:T(8,128)(2,1)S(1)}, u32[]{:S(2)}, u32[]{:S(2)}) collective-permute-start(bf16[8,256,128]{2,1,0:T(8,128)(2,1)S(1)} %get-tuple-element.228.refs_0_.ring_ref), channel_id=1, source_target_pairs={{0,2},{2,0},{1,3},{3,1},{4,6},{6,4},{5,7},{7,5},{8,10},{10,8},{9,1... | collective-permute-start | bytes 1572872 | tf_op jit(solution)/shard_map/ppermute | solution.py:1215
  97.7 13.6 %collective-permute-start.18 = (bf16[1024,256]{1,0:T(8,128)(2,1)S(1)}, bf16[1024,256]{1,0:T(8,128)(2,1)S(1)}, u32[]{:S(2)}, u32[]{:S(2)}) collective-permute-start(bf16[1024,256]{1,0:T(8,128)(2,1)S(1)} %get-tuple-element.230.own_ref.attn_ref), channel_id=1, source_target_pairs={{0,1},{1,0},{2,3},{3,2},{4,5},{5,4},{6,7},{7,6},{8,9},{9,8},{10,11... | collective-permute-start | bytes 1572872 | tf_op jit(solution)/shard_map/ppermute | solution.py:1210
  99.5 13.0 %collective-permute-start.23 = (bf16[2048,128]{1,0:T(8,128)(2,1)S(1)}, bf16[2048,128]{1,0:T(8,128)(2,1)S(1)}, u32[]{:S(2)}, u32[]{:S(2)}) collective-permute-start(bf16[2048,128]{1,0:T(8,128)(2,1)S(1)} %collective-permute-done.15), channel_id=1, source_target_pairs={{0,8},{8,16},{16,24},{24,28},{28,20},{20,12},{12,4},{4,0},{1,9},{9... | collective-permute-start | bytes 1572872 | tf_op jit(solution)/shard_map/ppermute | solution.py:1155
  99.5 13.0 %collective-permute-start.24 = (bf16[2048,128]{1,0:T(8,128)(2,1)S(1)}, bf16[2048,128]{1,0:T(8,128)(2,1)S(1)}, u32[]{:S(2)}, u32[]{:S(2)}) collective-permute-start(bf16[2048,128]{1,0:T(8,128)(2,1)S(1)} %collective-permute-done.16), channel_id=1, source_target_pairs={{8,0},{16,8},{24,16},{28,24},{20,28},{12,20},{4,12},{0,4},{9,1},{1... | collective-permute-start | bytes 1572872 | tf_op jit(solution)/shard_map/ppermute | solution.py:1155
  114.6 10.9 %collective-permute-start.25 = (bf16[1024,128]{1,0:T(8,128)(2,1)S(1)}, bf16[1024,128]{1,0:T(8,128)(2,1)S(1)}, u32[]{:S(2)}, u32[]{:S(2)}) collective-permute-start(bf16[1024,128]{1,0:T(8,128)(2,1)S(1)} %get-tuple-element.271.refs_0_), channel_id=1, source_target_pairs={{0,8},{8,16},{16,24},{24,28},{28,20},{20,12},{12,4},{4,0},{1,9},{9... | collective-permute-start | bytes 786440 | tf_op jit(solution)/shard_map/ppermute | solution.py:1155
  114.7 11.6 %collective-permute-start.26 = (bf16[1024,128]{1,0:T(8,128)(2,1)S(1)}, bf16[1024,128]{1,0:T(8,128)(2,1)}, u32[]{:S(2)}, u32[]{:S(2)}) collective-permute-start(bf16[1024,128]{1,0:T(8,128)(2,1)S(1)} %get-tuple-element.271.refs_0_), channel_id=1, source_target_pairs={{8,0},{16,8},{24,16},{28,24},{20,28},{12,20},{4,12},{0,4},{9,1},{1... | collective-permute-start | bytes 786440 | tf_op jit(solution)/shard_map/ppermute | solution.py:1155
  116.8 11.1 %collective-permute-start.27 = (bf16[1024,128]{1,0:T(8,128)(2,1)}, bf16[1024,128]{1,0:T(8,128)(2,1)}, u32[]{:S(2)}, u32[]{:S(2)}) collective-permute-start(bf16[1024,128]{1,0:T(8,128)(2,1)} %slice.70), channel_id=1, source_target_pairs={{0,8},{8,16},{16,24},{24,28},{28,20},{20,12},{12,4},{4,0},{1,9},{9... | collective-permute-start | bytes 786440 | tf_op jit(solution)/shard_map/ppermute | solution.py:1155
  117.6 11.1 %collective-permute-start.28 = (bf16[1024,128]{1,0:T(8,128)(2,1)}, bf16[1024,128]{1,0:T(8,128)(2,1)}, u32[]{:S(2)}, u32[]{:S(2)}) collective-permute-start(bf16[1024,128]{1,0:T(8,128)(2,1)} %slice.71), channel_id=1, source_target_pairs={{8,0},{16,8},{24,16},{28,24},{20,28},{12,20},{4,12},{0,4},{9,1},{1... | collective-permute-start | bytes 786440 | tf_op jit(solution)/shard_map/ppermute | solution.py:1155
  124.1 13.6 %collective-permute-start.31 = (bf16[256,1024]{1,0:T(8,128)(2,1)S(1)}, bf16[256,1024]{1,0:T(8,128)(2,1)}, u32[]{:S(2)}, u32[]{:S(2)}) collective-permute-start(bf16[256,1024]{1,0:T(8,128)(2,1)S(1)} %bitcast.130), channel_id=1, source_target_pairs={{0,2},{2,0},{1,3},{3,1},{4,6},{6,4},{5,7},{7,5},{8,10},{10,8},{9,1... | collective-permute-start | bytes 1572872 | tf_op jit(solution)/shard_map/ppermute | solution.py:1215
  126.3 11.4 %collective-permute-start.32 = (bf16[256,1024]{1,0:T(8,128)(2,1)}, bf16[256,1024]{1,0:T(8,128)(2,1)}, u32[]{:S(2)}, u32[]{:S(2)}) collective-permute-start(bf16[256,1024]{1,0:T(8,128)(2,1)} %collective-permute-done.14.pair_ref), channel_id=1, source_target_pairs={{0,2},{2,0},{1,3},{3,1},{4,6},{6,4},{5,7},{7,5},{8,10},{10,8},{9,1... | collective-permute-start | bytes 1572872 | tf_op jit(solution)/shard_map/ppermute | solution.py:1215
  126.3 9.8 %collective-permute-start.29 = (bf16[1024,128]{1,0:T(8,128)(2,1)}, bf16[1024,128]{1,0:T(8,128)(2,1)S(1)}, u32[]{:S(2)}, u32[]{:S(2)}) collective-permute-start(bf16[1024,128]{1,0:T(8,128)(2,1)} %copy-done.46), channel_id=1, source_target_pairs={{0,8},{8,16},{16,24},{24,28},{28,20},{20,12},{12,4},{4,0},{1,9},{9... | collective-permute-start | bytes 786440 | tf_op jit(solution)/shard_map/ppermute | solution.py:1155
  127.9 8.2 %collective-permute-start.30 = (bf16[1024,128]{1,0:T(8,128)(2,1)}, bf16[1024,128]{1,0:T(8,128)(2,1)S(1)}, u32[]{:S(2)}, u32[]{:S(2)}) collective-permute-start(bf16[1024,128]{1,0:T(8,128)(2,1)} %collective-permute-done.26.refs_2_), channel_id=1, source_target_pairs={{8,0},{16,8},{24,16},{28,24},{20,28},{12,20},{4,12},{0,4},{9,1},{1... | collective-permute-start | bytes 786440 | tf_op jit(solution)/shard_map/ppermute | solution.py:1155
  136.1 6.4 %collective-permute-start.33 = (bf16[1024,128]{1,0:T(8,128)(2,1)S(1)}, bf16[1024,128]{1,0:T(8,128)(2,1)S(1)}, u32[]{:S(2)}, u32[]{:S(2)}) collective-permute-start(bf16[1024,128]{1,0:T(8,128)(2,1)S(1)} %collective-permute-done.29.refs_3_), channel_id=1, source_target_pairs={{0,8},{8,16},{16,24},{24,28},{28,20},{20,12},{12,4},{4,0},{1,9},{9... | collective-permute-start | bytes 786440 | tf_op jit(solution)/shard_map/ppermute | solution.py:1155
  136.8 6.0 %collective-permute-start.34 = (bf16[1024,128]{1,0:T(8,128)(2,1)S(1)}, bf16[1024,128]{1,0:T(8,128)(2,1)S(1)}, u32[]{:S(2)}, u32[]{:S(2)}) collective-permute-start(bf16[1024,128]{1,0:T(8,128)(2,1)S(1)} %collective-permute-done.30.refs_4_), channel_id=1, source_target_pairs={{8,0},{16,8},{24,16},{28,24},{20,28},{12,20},{4,12},{0,4},{9,1},{1... | collective-permute-start | bytes 786440 | tf_op jit(solution)/shard_map/ppermute | solution.py:1155
  147.1 5.8 %collective-permute-start.37 = (bf16[512,128]{1,0:T(8,128)(2,1)S(1)}, bf16[512,128]{1,0:T(8,128)(2,1)S(1)}, u32[]{:S(2)}, u32[]{:S(2)}) collective-permute-start(bf16[512,128]{1,0:T(8,128)(2,1)S(1)} %get-tuple-element.274), channel_id=1, source_target_pairs={{0,8},{8,16},{16,24},{24,28},{28,20},{20,12},{12,4},{4,0},{1,9},{9... | collective-permute-start | bytes 393224 | tf_op jit(solution)/shard_map/ppermute | solution.py:1155
  147.3 5.6 %collective-permute-start.38 = (bf16[512,128]{1,0:T(8,128)(2,1)S(1)}, bf16[512,128]{1,0:T(8,128)(2,1)S(1)}, u32[]{:S(2)}, u32[]{:S(2)}) collective-permute-start(bf16[512,128]{1,0:T(8,128)(2,1)S(1)} %get-tuple-element.275), channel_id=1, source_target_pairs={{8,0},{16,8},{24,16},{28,24},{20,28},{12,20},{4,12},{0,4},{9,1},{1... | collective-permute-start | bytes 393224 | tf_op jit(solution)/shard_map/ppermute | solution.py:1155
  153.0 6.4 %collective-permute-start.39 = (bf16[1024,128]{1,0:T(8,128)(2,1)S(1)}, bf16[1024,128]{1,0:T(8,128)(2,1)S(1)}, u32[]{:S(2)}, u32[]{:S(2)}) collective-permute-start(bf16[1024,128]{1,0:T(8,128)(2,1)S(1)} %get-tuple-element.283), channel_id=1, source_target_pairs={{0,8},{8,16},{16,24},{24,28},{28,20},{20,12},{12,4},{4,0},{1,9},{9... | collective-permute-start | bytes 786440 | tf_op jit(solution)/shard_map/ppermute | solution.py:1155
  153.2 6.2 %collective-permute-start.40 = (bf16[1024,128]{1,0:T(8,128)(2,1)S(1)}, bf16[1024,128]{1,0:T(8,128)(2,1)S(1)}, u32[]{:S(2)}, u32[]{:S(2)}) collective-permute-start(bf16[1024,128]{1,0:T(8,128)(2,1)S(1)} %get-tuple-element.284), channel_id=1, source_target_pairs={{8,0},{16,8},{24,16},{28,24},{20,28},{12,20},{4,12},{0,4},{9,1},{1... | collective-permute-start | bytes 786440 | tf_op jit(solution)/shard_map/ppermute | solution.py:1155
  159.5 7.1 %collective-permute-start.42 = (bf16[256,1024]{1,0:T(8,128)(2,1)S(1)}, bf16[256,1024]{1,0:T(8,128)(2,1)S(1)}, u32[]{:S(2)}, u32[]{:S(2)}) collective-permute-start(bf16[256,1024]{1,0:T(8,128)(2,1)S(1)} %get-tuple-element.290), channel_id=1, source_target_pairs={{0,2},{2,0},{1,3},{3,1},{4,6},{6,4},{5,7},{7,5},{8,10},{10,8},{9,1... | collective-permute-start | bytes 1572872 | tf_op jit(solution)/shard_map/ppermute | solution.py:1220
  167.6 14.7 %collective-permute-start.43 = (bf16[256,1024]{1,0:T(8,128)(2,1)S(1)}, bf16[256,1024]{1,0:T(8,128)(2,1)S(1)}, u32[]{:S(2)}, u32[]{:S(2)}) collective-permute-start(bf16[256,1024]{1,0:T(8,128)(2,1)S(1)} %add_convert_fusion.3), channel_id=1, source_target_pairs={{0,1},{1,0},{2,3},{3,2},{4,5},{5,4},{6,7},{7,6},{8,9},{9,8},{10,11... | collective-permute-start | bytes 1572872 | tf_op jit(solution)/shard_map/ppermute | solution.py:1225
  173.8 8.0 %collective-permute-start.44 = (bf16[1024,128]{1,0:T(8,128)(2,1)S(1)}, bf16[1024,128]{1,0:T(8,128)(2,1)S(1)}, u32[]{:S(2)}, u32[]{:S(2)}) collective-permute-start(bf16[1024,128]{1,0:T(8,128)(2,1)S(1)} %get-tuple-element.393), channel_id=1, source_target_pairs={{0,8},{8,16},{16,24},{24,28},{28,20},{20,12},{12,4},{4,0},{1,9},{9... | collective-permute-start | bytes 786440 | tf_op jit(solution)/shard_map/ppermute | solution.py:1155
  175.3 7.0 %collective-permute-start.45 = (bf16[1024,128]{1,0:T(8,128)(2,1)S(1)}, bf16[1024,128]{1,0:T(8,128)(2,1)S(1)}, u32[]{:S(2)}, u32[]{:S(2)}) collective-permute-start(bf16[1024,128]{1,0:T(8,128)(2,1)S(1)} %get-tuple-element.392), channel_id=1, source_target_pairs={{8,0},{16,8},{24,16},{28,24},{20,28},{12,20},{4,12},{0,4},{9,1},{1... | collective-permute-start | bytes 786440 | tf_op jit(solution)/shard_map/ppermute | solution.py:1155
  176.7 16.9 %collective-permute-start.69 = (bf16[1024,128]{1,0:T(8,128)(2,1)S(1)}, bf16[1024,128]{1,0:T(8,128)(2,1)S(1)}, u32[]{:S(2)}, u32[]{:S(2)}) collective-permute-start(bf16[1024,128]{1,0:T(8,128)(2,1)S(1)} %get-tuple-element.360), channel_id=1, source_target_pairs={{0,8},{8,16},{16,24},{24,28},{28,20},{20,12},{12,4},{4,0},{1,9},{9... | collective-permute-start | bytes 786440 | tf_op jit(solution)/shard_map/ppermute | solution.py:1155
  177.6 19.7 %collective-permute-start.70 = (bf16[1024,128]{1,0:T(8,128)(2,1)}, bf16[1024,128]{1,0:T(8,128)(2,1)}, u32[]{:S(2)}, u32[]{:S(2)}) collective-permute-start(bf16[1024,128]{1,0:T(8,128)(2,1)} %get-tuple-element.361), channel_id=1, source_target_pairs={{8,0},{16,8},{24,16},{28,24},{20,28},{12,20},{4,12},{0,4},{9,1},{1... | collective-permute-start | bytes 786440 | tf_op jit(solution)/shard_map/ppermute | solution.py:1155
  183.8 16.5 %collective-permute-start.48 = (bf16[256,1024]{1,0:T(8,128)(2,1)S(1)}, bf16[256,1024]{1,0:T(8,128)(2,1)S(1)}, u32[]{:S(2)}, u32[]{:S(2)}) collective-permute-start(bf16[256,1024]{1,0:T(8,128)(2,1)S(1)} %multiply_convert_fusion.own_ref), channel_id=1, source_target_pairs={{0,1},{1,0},{2,3},{3,2},{4,5},{5,4},{6,7},{7,6},{8,9},{9,8},{10,11... | collective-permute-start | bytes 1572872 | tf_op jit(solution)/shard_map/ppermute | solution.py:1210
  185.7 13.1 %collective-permute-start.49 = (bf16[2048,128]{1,0:T(8,128)(2,1)}, bf16[2048,128]{1,0:T(8,128)(2,1)}, u32[]{:S(2)}, u32[]{:S(2)}) collective-permute-start(bf16[2048,128]{1,0:T(8,128)(2,1)} %pad_maximum_fusion.1), channel_id=1, source_target_pairs={{0,8},{8,16},{16,24},{24,28},{28,20},{20,12},{12,4},{4,0},{1,9},{9... | collective-permute-start | bytes 1572872 | tf_op jit(solution)/shard_map/ppermute | solution.py:1155
  186.7 13.2 %collective-permute-start.50 = (bf16[2048,128]{1,0:T(8,128)(2,1)}, bf16[2048,128]{1,0:T(8,128)(2,1)}, u32[]{:S(2)}, u32[]{:S(2)}) collective-permute-start(bf16[2048,128]{1,0:T(8,128)(2,1)} %pad_maximum_fusion.2), channel_id=1, source_target_pairs={{8,0},{16,8},{24,16},{28,24},{20,28},{12,20},{4,12},{0,4},{9,1},{1... | collective-permute-start | bytes 1572872 | tf_op jit(solution)/shard_map/ppermute | solution.py:1155
  193.5 8.9 %collective-permute-start.47 = (bf16[256,1024]{1,0:T(8,128)(2,1)}, bf16[256,1024]{1,0:T(8,128)(2,1)S(1)}, u32[]{:S(2)}, u32[]{:S(2)}) collective-permute-start(bf16[256,1024]{1,0:T(8,128)(2,1)} %get-tuple-element.302), channel_id=1, source_target_pairs={{0,2},{2,0},{1,3},{3,1},{4,6},{6,4},{5,7},{7,5},{8,10},{10,8},{9,1... | collective-permute-start | bytes 1572872 | tf_op jit(solution)/shard_map/ppermute | solution.py:1220
  197.3 6.8 %collective-permute-start.46 = (bf16[256,1024]{1,0:T(8,128)(2,1)S(1)}, bf16[256,1024]{1,0:T(8,128)(2,1)S(1)}, u32[]{:S(2)}, u32[]{:S(2)}) collective-permute-start(bf16[256,1024]{1,0:T(8,128)(2,1)S(1)} %get-tuple-element.300), channel_id=1, source_target_pairs={{0,2},{2,0},{1,3},{3,1},{4,6},{6,4},{5,7},{7,5},{8,10},{10,8},{9,1... | collective-permute-start | bytes 1572872 | tf_op jit(solution)/shard_map/ppermute | solution.py:1219
  198.8 44.1 %collective-permute-start.71 = (bf16[1024,128]{1,0:T(8,128)(2,1)S(1)}, bf16[1024,128]{1,0:T(8,128)(2,1)S(1)}, u32[]{:S(2)}, u32[]{:S(2)}) collective-permute-start(bf16[1024,128]{1,0:T(8,128)(2,1)S(1)} %get-tuple-element.405), channel_id=1, source_target_pairs={{0,8},{8,16},{16,24},{24,28},{28,20},{20,12},{12,4},{4,0},{1,9},{9... | collective-permute-start | bytes 786440 | tf_op jit(solution)/shard_map/ppermute | solution.py:1155
  199.9 43.0 %collective-permute-start.72 = (bf16[1024,128]{1,0:T(8,128)(2,1)S(1)}, bf16[1024,128]{1,0:T(8,128)(2,1)S(1)}, u32[]{:S(2)}, u32[]{:S(2)}) collective-permute-start(bf16[1024,128]{1,0:T(8,128)(2,1)S(1)} %get-tuple-element.404), channel_id=1, source_target_pairs={{8,0},{16,8},{24,16},{28,24},{20,28},{12,20},{4,12},{0,4},{9,1},{1... | collective-permute-start | bytes 786440 | tf_op jit(solution)/shard_map/ppermute | solution.py:1155
  200.4 6.3 %collective-permute-start.51 = (bf16[256,1024]{1,0:T(8,128)(2,1)S(1)}, bf16[256,1024]{1,0:T(8,128)(2,1)S(1)}, u32[]{:S(2)}, u32[]{:S(2)}) collective-permute-start(bf16[256,1024]{1,0:T(8,128)(2,1)S(1)} %multiply_convert_fusion.own_ref), channel_id=1, source_target_pairs={{0,2},{2,0},{1,3},{3,1},{4,6},{6,4},{5,7},{7,5},{8,10},{10,8},{9,1... | collective-permute-start | bytes 1572872 | tf_op jit(solution)/shard_map/ppermute | solution.py:1215
  206.7 14.6 %collective-permute-start.54 = (bf16[2048,128]{1,0:T(8,128)(2,1)S(1)}, bf16[2048,128]{1,0:T(8,128)(2,1)S(1)}, u32[]{:S(2)}, u32[]{:S(2)}) collective-permute-start(bf16[2048,128]{1,0:T(8,128)(2,1)S(1)} %get-tuple-element.324), channel_id=1, source_target_pairs={{0,8},{8,16},{16,24},{24,28},{28,20},{20,12},{12,4},{4,0},{1,9},{9... | collective-permute-start | bytes 1572872 | tf_op jit(solution)/shard_map/ppermute | solution.py:1155
  207.7 13.6 %collective-permute-start.55 = (bf16[2048,128]{1,0:T(8,128)(2,1)S(1)}, bf16[2048,128]{1,0:T(8,128)(2,1)S(1)}, u32[]{:S(2)}, u32[]{:S(2)}) collective-permute-start(bf16[2048,128]{1,0:T(8,128)(2,1)S(1)} %get-tuple-element.325), channel_id=1, source_target_pairs={{8,0},{16,8},{24,16},{28,24},{20,28},{12,20},{4,12},{0,4},{9,1},{1... | collective-permute-start | bytes 1572872 | tf_op jit(solution)/shard_map/ppermute | solution.py:1155
  208.4 21.8 %collective-permute-start.53 = (bf16[256,1024]{1,0:T(8,128)(2,1)S(1)}, bf16[256,1024]{1,0:T(8,128)(2,1)S(1)}, u32[]{:S(2)}, u32[]{:S(2)}) collective-permute-start(bf16[256,1024]{1,0:T(8,128)(2,1)S(1)} %add_convert_fusion.2), channel_id=1, source_target_pairs={{0,1},{1,0},{2,3},{3,2},{4,5},{5,4},{6,7},{7,6},{8,9},{9,8},{10,11... | collective-permute-start | bytes 1572872 | tf_op jit(solution)/shard_map/ppermute | solution.py:1225
  221.6 12.2 %collective-permute-start.59 = (bf16[2048,128]{1,0:T(8,128)(2,1)S(1)}, bf16[2048,128]{1,0:T(8,128)(2,1)S(1)}, u32[]{:S(2)}, u32[]{:S(2)}) collective-permute-start(bf16[2048,128]{1,0:T(8,128)(2,1)S(1)} %get-tuple-element.339), channel_id=1, source_target_pairs={{0,8},{8,16},{16,24},{24,28},{28,20},{20,12},{12,4},{4,0},{1,9},{9... | collective-permute-start | bytes 1572872 | tf_op jit(solution)/shard_map/ppermute | solution.py:1155
  222.7 13.3 %collective-permute-start.60 = (bf16[2048,128]{1,0:T(8,128)(2,1)S(1)}, bf16[2048,128]{1,0:T(8,128)(2,1)S(1)}, u32[]{:S(2)}, u32[]{:S(2)}) collective-permute-start(bf16[2048,128]{1,0:T(8,128)(2,1)S(1)} %get-tuple-element.340), channel_id=1, source_target_pairs={{8,0},{16,8},{24,16},{28,24},{20,28},{12,20},{4,12},{0,4},{9,1},{1... | collective-permute-start | bytes 1572872 | tf_op jit(solution)/shard_map/ppermute | solution.py:1155
  230.2 7.0 %collective-permute-start.57 = (bf16[256,1024]{1,0:T(8,128)(2,1)S(1)}, bf16[256,1024]{1,0:T(8,128)(2,1)S(1)}, u32[]{:S(2)}, u32[]{:S(2)}) collective-permute-start(bf16[256,1024]{1,0:T(8,128)(2,1)S(1)} %get-tuple-element.335), channel_id=1, source_target_pairs={{0,2},{2,0},{1,3},{3,1},{4,6},{6,4},{5,7},{7,5},{8,10},{10,8},{9,1... | collective-permute-start | bytes 1572872 | tf_op jit(solution)/shard_map/ppermute | solution.py:1220
  236.0 5.2 %collective-permute-start.61 = (bf16[528,128]{1,0:T(8,128)(2,1)S(1)}, bf16[528,128]{1,0:T(8,128)(2,1)S(1)}, u32[]{:S(2)}, u32[]{:S(2)}) collective-permute-start(bf16[528,128]{1,0:T(8,128)(2,1)S(1)} %get-tuple-element.346), channel_id=1, source_target_pairs={{0,8},{8,16},{16,24},{24,28},{28,20},{20,12},{12,4},{4,0},{1,9},{9... | collective-permute-start | bytes 405512 | tf_op jit(solution)/shard_map/ppermute | solution.py:1155
  241.4 5.8 %collective-permute-start.63 = (bf16[1040,128]{1,0:T(8,128)(2,1)S(1)}, bf16[1040,128]{1,0:T(8,128)(2,1)S(1)}, u32[]{:S(2)}, u32[]{:S(2)}) collective-permute-start(bf16[1040,128]{1,0:T(8,128)(2,1)S(1)} %pad_maximum_fusion.3), channel_id=1, source_target_pairs={{0,8},{8,16},{16,24},{24,28},{28,20},{20,12},{12,4},{4,0},{1,9},{9... | collective-permute-start | bytes 798728 | tf_op jit(solution)/shard_map/ppermute | solution.py:1155
  242.3 5.6 %collective-permute-start.64 = (bf16[1040,128]{1,0:T(8,128)(2,1)S(1)}, bf16[1040,128]{1,0:T(8,128)(2,1)S(1)}, u32[]{:S(2)}, u32[]{:S(2)}) collective-permute-start(bf16[1040,128]{1,0:T(8,128)(2,1)S(1)} %pad_maximum_fusion.4), channel_id=1, source_target_pairs={{8,0},{16,8},{24,16},{28,24},{20,28},{12,20},{4,12},{0,4},{9,1},{1... | collective-permute-start | bytes 798728 | tf_op jit(solution)/shard_map/ppermute | solution.py:1155
  242.9 10.8 %collective-permute-start.58 = (bf16[256,1024]{1,0:T(8,128)(2,1)S(1)}, bf16[256,1024]{1,0:T(8,128)(2,1)S(1)}, u32[]{:S(2)}, u32[]{:S(2)}) collective-permute-start(bf16[256,1024]{1,0:T(8,128)(2,1)S(1)} %add_convert_fusion), channel_id=1, source_target_pairs={{0,1},{1,0},{2,3},{3,2},{4,5},{5,4},{6,7},{7,6},{8,9},{9,8},{10,11... | collective-permute-start | bytes 1572872 | tf_op jit(solution)/shard_map/ppermute | solution.py:1225
  248.0 7.5 %collective-permute-start.65 = (bf16[1040,128]{1,0:T(8,128)(2,1)S(1)}, bf16[1040,128]{1,0:T(8,128)(2,1)S(1)}, u32[]{:S(2)}, u32[]{:S(2)}) collective-permute-start(bf16[1040,128]{1,0:T(8,128)(2,1)S(1)} %get-tuple-element.399), channel_id=1, source_target_pairs={{0,8},{8,16},{16,24},{24,28},{28,20},{20,12},{12,4},{4,0},{1,9},{9... | collective-permute-start | bytes 798728 | tf_op jit(solution)/shard_map/ppermute | solution.py:1155
  249.5 6.0 %collective-permute-start.66 = (bf16[1040,128]{1,0:T(8,128)(2,1)S(1)}, bf16[1040,128]{1,0:T(8,128)(2,1)S(1)}, u32[]{:S(2)}, u32[]{:S(2)}) collective-permute-start(bf16[1040,128]{1,0:T(8,128)(2,1)S(1)} %get-tuple-element.398), channel_id=1, source_target_pairs={{8,0},{16,8},{24,16},{28,24},{20,28},{12,20},{4,12},{0,4},{9,1},{1... | collective-permute-start | bytes 798728 | tf_op jit(solution)/shard_map/ppermute | solution.py:1155
  255.6 5.3 %collective-permute-start.67 = (bf16[1040,128]{1,0:T(8,128)(2,1)S(1)}, bf16[1040,128]{1,0:T(8,128)(2,1)S(1)}, u32[]{:S(2)}, u32[]{:S(2)}) collective-permute-start(bf16[1040,128]{1,0:T(8,128)(2,1)S(1)} %get-tuple-element.356), channel_id=1, source_target_pairs={{0,8},{8,16},{16,24},{24,28},{28,20},{20,12},{12,4},{4,0},{1,9},{9... | collective-permute-start | bytes 798728 | tf_op jit(solution)/shard_map/ppermute | solution.py:1155
  257.1 5.3 %collective-permute-start.68 = (bf16[1040,128]{1,0:T(8,128)(2,1)S(1)}, bf16[1040,128]{1,0:T(8,128)(2,1)S(1)}, u32[]{:S(2)}, u32[]{:S(2)}) collective-permute-start(bf16[1040,128]{1,0:T(8,128)(2,1)S(1)} %get-tuple-element.357), channel_id=1, source_target_pairs={{8,0},{16,8},{24,16},{28,24},{20,28},{12,20},{4,12},{0,4},{9,1},{1... | collective-permute-start | bytes 798728 | tf_op jit(solution)/shard_map/ppermute | solution.py:1155
  (61 other events, 914.0 us)
